TPU v7x, 32 devices: a whole 2x2x4 slice. The times are simulated.
32 devices in a mesh: det: 8 (over z, y), tm: 4 (over x, core).
Axes of the slice: x: 2, y: 2, z: 4, core: 2. Of those that a mesh axis runs over, the one named last changes fastest.
Arguments:
- timestreams: float32 [2048, 24000], P('det', 'tm'), may hold values from -6 to 6
- wafer_group: int32 [2048], P('det'), may hold values from 0 to 11
- valid_blocks: int32 [2048, 200], P('det', 'tm'), may hold values 0 or 1
- gain_guess: float32 [2048], P('det'), may hold values from 0.5 to 2
- inverse_psd: float32 [12, 24000], replicated, may hold values from 0.05 to 1
Outputs:
- filtered: float32 [2048, 24000], P('det', 'tm')
- gains: float32 [2048], P('det')
- template: float32 [12, 24000], P(None, 'tm')
All inputs are finite; a program needn't handle non-finite values. No bound on the sum of `valid_blocks` on one device may be relied on, other than what follows from the above.
Results may differ from a plain program's by a relative error of at most 0.00027.
Values sent between devices are 32-bit elements; how exact they have to be, the bound alone decides.
A program may use at most 128 MiB of HBM per device.

v0:
```python
import math

import jax
import jax.numpy as jnp
from jax import lax
from jax.sharding import PartitionSpec as P

P_SIZE = 120
Q = 200
ITERS = 3


def tables(first, second, total):
    first_idx = jnp.arange(first, dtype=jnp.int32)
    second_idx = jnp.arange(second, dtype=jnp.int32)
    phase = first_idx[:, None] * second_idx[None, :] % total
    angle = phase.astype(jnp.float32) * (2.0 * math.pi / total)
    return (jnp.cos(angle), jnp.sin(angle))


def filter_rows(rows, weights):
    highest = lax.Precision.HIGHEST
    length = P_SIZE * Q
    count = rows.shape[0]
    cos_p, sin_p = tables(P_SIZE, P_SIZE, P_SIZE)
    cos_q, sin_q = tables(Q, Q, Q)
    cos_t, sin_t = tables(P_SIZE, Q, length)
    signal = rows.reshape(count, P_SIZE, Q)
    first_re = jnp.einsum("kp,rpq->rkq", cos_p, signal, precision=highest)
    first_im = -jnp.einsum("kp,rpq->rkq", sin_p, signal, precision=highest)
    twist_re = first_re * cos_t + first_im * sin_t
    twist_im = first_im * cos_t - first_re * sin_t
    freq_re = jnp.einsum("rkq,qj->rkj", twist_re, cos_q, precision=highest) + jnp.einsum(
        "rkq,qj->rkj", twist_im, sin_q, precision=highest
    )
    freq_im = jnp.einsum("rkq,qj->rkj", twist_im, cos_q, precision=highest) - jnp.einsum(
        "rkq,qj->rkj", twist_re, sin_q, precision=highest
    )
    factor = jnp.transpose(weights.reshape(count, Q, P_SIZE), (0, 2, 1))
    freq_re = freq_re * factor
    freq_im = freq_im * factor
    back_re = jnp.einsum("rkj,jq->rkq", freq_re, cos_q, precision=highest) - jnp.einsum(
        "rkj,jq->rkq", freq_im, sin_q, precision=highest
    )
    back_im = jnp.einsum("rkj,jq->rkq", freq_im, cos_q, precision=highest) + jnp.einsum(
        "rkj,jq->rkq", freq_re, sin_q, precision=highest
    )
    turn_re = back_re * cos_t - back_im * sin_t
    turn_im = back_im * cos_t + back_re * sin_t
    result = jnp.einsum("pk,rkq->rpq", cos_p, turn_re, precision=highest) - jnp.einsum(
        "pk,rkq->rpq", sin_p, turn_im, precision=highest
    )
    return (result / length).reshape(count, length)


def local(timestreams, wafer_group, valid_blocks, gain_guess, inverse_psd):
    highest = lax.Precision.HIGHEST
    det_rows, samp_dev = timestreams.shape
    groups = inverse_psd.shape[0]
    block = samp_dev // valid_blocks.shape[1]
    mask = jnp.repeat(valid_blocks.astype(jnp.float32), block, axis=1)
    onehot = (wafer_group[:, None] == jnp.arange(groups, dtype=jnp.int32)[None, :]).astype(
        jnp.float32
    )
    counts = lax.psum(jnp.sum(onehot, axis=0), "det")
    masked = mask * timestreams
    gains = gain_guess
    template = jnp.zeros((groups, samp_dev), jnp.float32)
    per_det = jnp.zeros_like(masked)
    for rounds in range(ITERS):
        squares = lax.psum(jnp.dot(gains * gains, onehot, precision=highest), "det")
        scale = jnp.sqrt(squares / jnp.maximum(counts, 1.0) + 1e-05)
        normed = gains / jnp.dot(onehot, scale, precision=highest)
        sum_one, sum_two = lax.psum(
            (
                jnp.dot(onehot.T, masked * normed[:, None], precision=highest),
                jnp.dot(onehot.T, mask * (normed * normed)[:, None], precision=highest),
            ),
            "det",
        )
        template = sum_one / (1.0 + sum_two)
        per_det = jnp.dot(onehot, template, precision=highest)
        numer, denom = lax.psum(
            (jnp.sum(masked * per_det, axis=1), jnp.sum(mask * per_det * per_det, axis=1)), "tm"
        )
        gains = numer / (1.0 + denom)
    local_count = det_rows // lax.axis_size("tm")
    offset = lax.axis_index("tm") * local_count
    local_hot = lax.dynamic_slice_in_dim(onehot, offset, local_count, 0)
    cleaned = masked - gains[:, None] * mask * per_det
    rows = lax.all_to_all(cleaned, "tm", split_axis=0, concat_axis=1, tiled=True)
    weights = jnp.dot(local_hot, inverse_psd, precision=highest)
    filtered_rows = filter_rows(rows, weights)
    filtered = lax.all_to_all(filtered_rows, "tm", split_axis=1, concat_axis=0, tiled=True)
    return (filtered, gains, template)


def solution(mesh):
    in_specs = (P("det", "tm"), P("det"), P("det", "tm"), P("det"), P())
    out_specs = (P("det", "tm"), P("det"), P(None, "tm"))
    return jax.shard_map(local, mesh=mesh, in_specs=in_specs, out_specs=out_specs, check_vma=False)
```

profile of v0, /device:TPU:13, one launch (start us, length us, event | category | flops | bytes accessed | tf_op | source)
XLA Modules:
  0.0 727.2 jit_solution(12082686067751941850)
XLA Ops:
  7.2 0.0 all-reduce.15.cloned.1.call-start
  7.2 0.9 convert_reduce_fusion
  8.1 0.8 mul.388
  8.9 0.8 convolution_bitcast_fusion.2
  9.7 11.6 %all-reduce = (f32[12]{0:T(128)S(1)}, f32[12]{0:T(128)S(1)}) all-reduce(f32[12]{0:T(128)S(1)} %convolution_bitcast_fusion.2, f32[12]{0:T(128)S(1)} %convert_reduce_fusion), channel_id=1, replica_groups=mesh['det'=8,'tm'=4] {'det'}, use_global_device_ids=true, to_apply=%region_0.0 | all-reduce | flops 24 | bytes 192 | tf_op jit(solution)/shard_map/psum | solution.py:71
  21.3 0.8 fusion.144
  22.1 0.7 fusion.218
  22.8 0.8 convert_element_type.56
  23.6 3.7 bitcast_multiply_fusion.6
  27.3 3.6 fusion.143
  31.0 3.8 fusion.22
  34.7 0.0 all-reduce.15.cloned.1.call-update
  34.8 0.0 all-reduce.13.cloned.1.call-start
  34.8 80.2 %all-reduce.15.cloned.1.call-done = (f32[12,6000]{1,0:T(8,128)}, f32[12,6000]{1,0:T(8,128)}) async-done(((f32[12,6000]{1,0:T(8,128)}, f32[12,6000]{1,0:T(8,128)}), (f32[12,6000]{1,0:T(8,128)}, f32[12,6000]{1,0:T(8,128)})) %all-reduce.15.cloned.1.call-update) | async-done | bytes 576016 | tf_op jit(solution)/shard_map/psum | solution.py:74
  115.0 6.4 fusion.15
  121.4 6.7 all-reduce.6
  128.1 0.1 convolution_bitcast_fusion.1
  128.2 12.5 %psum.118 = f32[12]{0:T(128)S(1)} all-reduce(f32[12]{0:T(128)S(1)} %convolution_bitcast_fusion.1), channel_id=1, replica_groups=mesh['det'=8,'tm'=4] {'det'}, use_global_device_ids=true, to_apply=%region_9.0 | all-reduce | flops 12 | bytes 96 | tf_op jit(solution)/shard_map/psum | solution.py:71
  140.7 0.1 fusion.142
  140.8 6.5 fusion.20
  147.3 0.4 bitcast_multiply_fusion.4
  147.7 3.6 fusion.141
  151.4 0.0 all-reduce.13.cloned.1.call-update
  151.4 0.0 all-reduce.11.cloned.1.call-start
  151.5 78.6 %all-reduce.13.cloned.1.call-done = (f32[12,6000]{1,0:T(8,128)}, f32[12,6000]{1,0:T(8,128)}) async-done(((f32[12,6000]{1,0:T(8,128)}, f32[12,6000]{1,0:T(8,128)}), (f32[12,6000]{1,0:T(8,128)}, f32[12,6000]{1,0:T(8,128)})) %all-reduce.13.cloned.1.call-update) | async-done | bytes 576016 | tf_op jit(solution)/shard_map/psum | solution.py:74
  230.0 6.4 fusion.14
  236.4 6.7 all-reduce.5
  243.1 0.1 convolution_bitcast_fusion
  243.2 12.7 %psum.123 = f32[12]{0:T(128)S(1)} all-reduce(f32[12]{0:T(128)S(1)} %convolution_bitcast_fusion), channel_id=1, replica_groups=mesh['det'=8,'tm'=4] {'det'}, use_global_device_ids=true, to_apply=%region_16.0 | all-reduce | flops 12 | bytes 96 | tf_op jit(solution)/shard_map/psum | solution.py:71
  255.9 0.1 fusion.140
  256.0 6.5 fusion.18
  262.6 0.4 bitcast_multiply_fusion.2
  263.0 3.6 fusion.139
  266.6 0.0 all-reduce.11.cloned.1.call-update
  266.6 78.6 %all-reduce.11.cloned.1.call-done = (f32[12,6000]{1,0:T(8,128)}, f32[12,6000]{1,0:T(8,128)}) async-done(((f32[12,6000]{1,0:T(8,128)}, f32[12,6000]{1,0:T(8,128)}), (f32[12,6000]{1,0:T(8,128)}, f32[12,6000]{1,0:T(8,128)})) %all-reduce.11.cloned.1.call-update) | async-done | bytes 576016 | tf_op jit(solution)/shard_map/psum | solution.py:74
  345.3 1.2 add_divide_fusion
  346.5 8.9 %fusion.13 = (f32[256]{0:T(256)S(1)}, f32[256]{0:T(256)S(1)}, f32[256,6000]{0,1:T(8,128)}) fusion(f32[256,50]{0,1:T(8,128)S(1)} %convert_element_type.56, f32[256,6000]{0,1:T(8,128)} %param.5, f32[12,6000]{1,0:T(8,128)S(1)} %add_divide_fusion, s32[256]{0:T(256)S(1)} %copy-done.7), kind=kOutput, calls=%fused_computation.28 | convolution fusion | flops 230402560 | bytes 12630272 | tf_op jit(solution)/shard_map/dot_general | solution.py:82
  355.3 6.6 all-reduce.4
  362.0 8.0 %fusion.17 = f32[256,6000]{0,1:T(8,128)} fusion(f32[256,6000]{0,1:T(8,128)} %get-tuple-element.40, f32[256,6000]{0,1:T(8,128)} %param.5, f32[256]{0:T(256)S(1)} %add_divide_fusion.1, f32[256,50]{0,1:T(8,128)S(1)} %convert_element_type.56), kind=kLoop, calls=%fused_computation.32 | loop fusion | flops 6144000 | bytes 18484224 | tf_op jit(solution)/shard_map/sub | solution.py:90
  370.0 6.5 copy.22
  376.5 6.0 all-to-all-start
  382.6 5.2 fusion.160
  387.8 7.7 %reshape.65 = f32[64,200,120]{2,1,0:T(8,128)} reshape(f32[64,24000]{1,0:T(8,128)} %fusion.160) | data formatting | bytes 12288000 | tf_op jit(solution)/shard_map/reshape | solution.py:39
  395.4 0.4 fusion.106
  395.9 55.1 %all-to-all-done = f32[4,64,6000]{2,1,0:T(8,128)} async-done(((f32[4,64,6000]{2,1,0:T(8,128)}), f32[4,64,6000]{2,1,0:T(8,128)}, u32[]{:S(2)}, u32[]{:S(2)}) %all-to-all-start) | async-done | bytes 6144032 | tf_op jit(solution)/shard_map/all_to_all | solution.py:91
  451.0 9.3 %copy.23 = f32[64,4,6000]{2,1,0:T(4,128)} copy(f32[64,4,6000]{2,0,1:T(8,128)} %bitcast.14) | data formatting | bytes 12288000 | tf_op jit(solution)/shard_map/all_to_all | solution.py:91
  460.2 10.0 %reshape.64 = f32[64,120,200]{2,1,0:T(8,128)} reshape(f32[64,4,6000]{2,1,0:T(4,128)} %copy.23) | data formatting | bytes 12288000 | tf_op jit(solution)/shard_map/reshape | solution.py:28
  470.2 17.2 %fusion.112 = f32[64,200,120]{2,1,0:T(8,128)S(1)} fusion(f32[64,120,200]{2,1,0:T(8,128)} %reshape.64), kind=kOutput, calls=%fused_computation.117 | convolution fusion | flops 2211969536 | bytes 12288000 | tf_op jit(solution)/shard_map/kp,rpq->rkq/dot_general | solution.py:30
  487.4 13.7 %fusion.115 = f32[64,200,120]{2,1,0:T(8,128)S(1)} fusion(f32[64,120,200]{2,1,0:T(8,128)S(1)} %copy-done.3), kind=kOutput, calls=%fused_computation.120 | convolution fusion | flops 2211969536 | bytes 12288000 | tf_op jit(solution)/shard_map/kp,rpq->rkq/dot_general | solution.py:29
  501.1 10.4 %fusion.37 = f32[64,120,200]{1,2,0:T(8,128)} fusion(f32[64,200,120]{2,1,0:T(8,128)S(1)} %fusion.115, f32[64,200,120]{2,1,0:T(8,128)S(1)} %fusion.112, f32[120,200]{0,1:T(8,128)S(1)} %get-tuple-element.41, f32[120,200]{0,1:T(8,128)S(1)} %get-tuple-element.42), kind=kOutput, calls=%fused_computation.53 | convolution fusion | flops 3692903936 | bytes 18624000 | tf_op jit(solution)/shard_map/rkq,qj->rkj/dot_general | solution.py:36
  511.5 14.0 %bitcast_multiply_fusion.8 = f32[64,120,200]{1,2,0:T(8,128)} fusion(f32[64,200,120]{2,1,0:T(8,128)} %reshape.65, f32[64,120,200]{1,2,0:T(8,128)} %fusion.37, f32[64,200,120]{2,1,0:T(8,128)S(1)} %fusion.115, f32[64,200,120]{2,1,0:T(8,128)S(1)} %fusion.112, f32[120,200]{0,1:T(8,128)S(1)} %get-tuple-element.41, f32[120,200]{0,1:T(8,128)S(1)} %get-tuple-element.42), kind=kOutput, calls=%fused_computation.11 | convolution fusion | flops 3695975936 | bytes 30912000 | tf_op jit(solution)/shard_map/rkq,qj->rkj/dot_general | solution.py:36
  525.5 12.2 %fusion.57 = f32[64,120,200]{1,2,0:T(8,128)} fusion(f32[64,120,200]{1,2,0:T(8,128)} %bitcast_multiply_fusion.8), kind=kOutput, calls=%fused_computation.74 | convolution fusion | flops 3686759936 | bytes 12288000 | tf_op jit(solution)/shard_map/rkj,jq->rkq/dot_general | solution.py:45
  537.8 9.5 %fusion.53 = f32[64,120,200]{1,2,0:T(8,128)} fusion(f32[64,120,200]{1,2,0:T(8,128)S(1)} %copy-done.5), kind=kOutput, calls=%fused_computation.70 | convolution fusion | flops 3686759936 | bytes 12288000 | tf_op jit(solution)/shard_map/rkj,jq->rkq/dot_general | solution.py:42
  547.2 10.8 %fusion.41 = f32[64,120,200]{1,2,0:T(8,128)} fusion(f32[64,200,120]{2,1,0:T(8,128)S(1)} %fusion.115, f32[64,200,120]{2,1,0:T(8,128)S(1)} %fusion.112, f32[120,200]{0,1:T(8,128)S(1)} %get-tuple-element.41, f32[120,200]{0,1:T(8,128)S(1)} %get-tuple-element.42), kind=kOutput, calls=%fused_computation.54 | convolution fusion | flops 3692903936 | bytes 18624000 | tf_op jit(solution)/shard_map/rkq,qj->rkj/dot_general | solution.py:33
  558.1 13.9 %bitcast_multiply_fusion.9 = f32[64,120,200]{1,2,0:T(8,128)} fusion(f32[64,200,120]{2,1,0:T(8,128)} %reshape.65, f32[64,120,200]{1,2,0:T(8,128)} %fusion.41, f32[64,200,120]{2,1,0:T(8,128)S(1)} %fusion.115, f32[64,200,120]{2,1,0:T(8,128)S(1)} %fusion.112, f32[120,200]{0,1:T(8,128)S(1)} %get-tuple-element.41, f32[120,200]{0,1:T(8,128)S(1)} %get-tuple-element.42), kind=kOutput, calls=%fused_computation.12 | convolution fusion | flops 3695975936 | bytes 30912000 | tf_op jit(solution)/shard_map/rkq,qj->rkj/dot_general | solution.py:33
  572.0 12.2 %fusion.51 = f32[64,120,200]{1,2,0:T(8,128)} fusion(f32[64,120,200]{1,2,0:T(8,128)} %bitcast_multiply_fusion.9), kind=kOutput, calls=%fused_computation.68 | convolution fusion | flops 3686759936 | bytes 12288000 | tf_op jit(solution)/shard_map/rkj,jq->rkq/dot_general | solution.py:45
  584.1 9.4 %fusion.60 = f32[64,120,200]{1,2,0:T(8,128)} fusion(f32[64,120,200]{1,2,0:T(8,128)S(1)} %copy-done.4), kind=kOutput, calls=%fused_computation.77 | convolution fusion | flops 3686759936 | bytes 12288000 | tf_op jit(solution)/shard_map/rkj,jq->rkq/dot_general | solution.py:42
  593.6 12.3 %fusion.5 = f32[64,200,120]{2,1,0:T(8,128)} fusion(f32[120,200]{0,1:T(8,128)S(1)} %get-tuple-element.41, f32[120,200]{0,1:T(8,128)S(1)} %get-tuple-element.42, f32[64,120,200]{1,2,0:T(8,128)S(1)} %bitcast.129, f32[64,120,200]{1,2,0:T(8,128)} %fusion.51, f32[64,120,200]{1,2,0:T(8,128)} %fusion.60, f32[64,120,200]{1,2,0:T(8,128)} %fusion.53), kind=kOutput, calls=%fused_computation.20 | convolution fusion | flops 2219649536 | bytes 30912000 | tf_op jit(solution)/shard_map/pk,rkq->rpq/dot_general | solution.py:50
  605.9 13.8 %multiply_bitcast_fusion = f32[64,120,200]{1,2,0:T(8,128)} fusion(f32[64,200,120]{2,1,0:T(8,128)} %fusion.5, f32[120,200]{0,1:T(8,128)S(1)} %get-tuple-element.41, f32[120,200]{0,1:T(8,128)S(1)} %get-tuple-element.42, f32[64,120,200]{1,2,0:T(8,128)S(1)} %bitcast.129, f32[64,120,200]{1,2,0:T(8,128)} %fusion.51, f32[64,120,200]{1,2,0:T(8,128)} %fusion.60, ...), kind=kOutput, calls=%fused_computation.19 | convolution fusion | flops 2222721536 | bytes 37056000 | tf_op jit(solution)/shard_map/pk,rkq->rpq/dot_general | solution.py:50
  619.7 8.5 %copy.26 = f32[64,120,200]{2,1,0:T(8,128)} copy(f32[64,120,200]{1,2,0:T(8,128)} %multiply_bitcast_fusion) | data formatting | bytes 12288000 | tf_op jit(solution)/shard_map/div | solution.py:53
  628.2 9.7 %all_to_all.29 = f32[64,4,6000]{2,1,0:T(4,128)} reshape(f32[64,120,200]{2,1,0:T(8,128)} %copy.26) | data formatting | bytes 12288000 | tf_op jit(solution)/shard_map/all_to_all | solution.py:94
  637.9 3.2 copy.27
  641.1 72.8 %all_to_all.35 = f32[64,4,6000]{2,0,1:T(8,128)} all-to-all(f32[64,4,6000]{2,0,1:T(8,128)S(1)} %copy.27), channel_id=1, replica_groups=mesh['det'=8,'tm'=4] {'tm'}, dimensions={1} | all-to-all | bytes 12288000 | tf_op jit(solution)/shard_map/all_to_all | solution.py:94
  713.9 6.5 copy.28
  (29 shorter events, 0.1 us)
Async XLA Ops:
  7.2 375.4 %copy-start = (f32[12,24000]{1,0:T(8,128)S(1)}, f32[12,24000]{1,0:T(8,128)}, u32[]{:S(2)}) copy-start(f32[12,24000]{1,0:T(8,128)} %param.9) | copy-start | bytes 3456004
  7.2 107.8 %all-reduce.15.cloned.1.call-start = ((), (), s32[]{:S(2)}) async-start(), calls=%async_computation.4 | async-start | bytes 1540096 | tf_op jit(solution)/shard_map/psum | solution.py:74
  23.6 3.7 copy-start.7
  27.3 3.7 copy-start.2
  34.8 195.2 %all-reduce.13.cloned.1.call-start = ((), (), s32[]{:S(2)}) async-start(), calls=%async_computation.3 | async-start | bytes 1540096 | tf_op jit(solution)/shard_map/psum | solution.py:74
  151.4 193.9 %all-reduce.11.cloned.1.call-start = ((), (), s32[]{:S(2)}) async-start(), calls=%async_computation.2 | async-start | bytes 1540096 | tf_op jit(solution)/shard_map/psum | solution.py:74
  346.4 23.6 %copy-start.6 = (f32[12,6000]{1,0:T(8,128)}, f32[12,6000]{1,0:T(8,128)S(1)}, u32[]{:S(2)}) copy-start(f32[12,6000]{1,0:T(8,128)S(1)} %add_divide_fusion) | copy-start | bytes 864004
  362.0 8.0 %copy-start.8 = (f32[256]{0:T(256)}, f32[256]{0:T(256)S(1)}, u32[]{:S(2)}) copy-start(f32[256]{0:T(256)S(1)} %add_divide_fusion.1) | copy-start | bytes 3076
  376.5 74.4 %all-to-all-start = ((f32[4,64,6000]{2,1,0:T(8,128)}), f32[4,64,6000]{2,1,0:T(8,128)}, u32[]{:S(2)}, u32[]{:S(2)}) async-start(f32[4,64,6000]{2,1,0:T(8,128)} %bitcast.130), calls=%async_computation | async-start | bytes 12320768 | tf_op jit(solution)/shard_map/all_to_all | solution.py:91
  470.2 17.2 %copy-start.3 = (f32[64,120,200]{2,1,0:T(8,128)S(1)}, f32[64,120,200]{2,1,0:T(8,128)}, u32[]{:S(2)}) copy-start(f32[64,120,200]{2,1,0:T(8,128)} %reshape.64) | copy-start | bytes 18432004
  525.5 12.2 %copy-start.5 = (f32[64,120,200]{1,2,0:T(8,128)S(1)}, f32[64,120,200]{1,2,0:T(8,128)}, u32[]{:S(2)}) copy-start(f32[64,120,200]{1,2,0:T(8,128)} %bitcast_multiply_fusion.8) | copy-start | bytes 18432004
  572.0 12.2 %copy-start.4 = (f32[64,120,200]{1,2,0:T(8,128)S(1)}, f32[64,120,200]{1,2,0:T(8,128)}, u32[]{:S(2)}) copy-start(f32[64,120,200]{1,2,0:T(8,128)} %bitcast_multiply_fusion.9) | copy-start | bytes 18432004
  572.0 21.6 %slice-start = ((s8[6553600]{0:T(1024)(128)(4,1)}), s8[4194304]{0:T(1024)(128)(4,1)S(1)}, s32[]{:S(2)}) async-start(s8[6553600]{0:T(1024)(128)(4,1)} %bitcast.128), calls=%async_computation.5 | async-start | bytes 8388608
  584.1 9.4 %slice-start.1 = ((s8[6553600]{0:T(1024)(128)(4,1)}), s8[2359296]{0:T(1024)(128)(4,1)S(1)}, s32[]{:S(2)}) async-start(s8[6553600]{0:T(1024)(128)(4,1)} %bitcast.128), calls=%async_computation.6 | async-start | bytes 4718592
  641.1 79.3 %copy-start.1 = (f32[12,24000]{1,0:T(8,128)S(1)}, f32[12,24000]{1,0:T(8,128)}, u32[]{:S(2)}) copy-start(f32[12,24000]{1,0:T(8,128)} %param.9) | copy-start | bytes 3456004
Sparse Core Ops, SparseCore 0:
  34.9 80.0 all-reduce.14
  151.5 78.4 all-reduce.12
  266.8 78.4 all-reduce.10
where the time goes:
time: 739 us; the launch traced here: 727 us
  waiting for transfers between devices  293 us (40%)
  matrix products  206 us (28%)
  blocking collectives  130 us (18%)
  local copies, waits for them, and re-layouts  61.3 us (8%)
  other arithmetic  17.3 us (2%)
  between operations  14.1 us (2%)
    psum x3, waiting for transfers between devices, local(): lax.psum((jnp.dot(onehot.T, masked * normed[:, None], precision=highest),...  237 us
    all_to_all x1, blocking collectives, local(): lax.all_to_all(filtered_rows, 'tm', split_axis=1, concat_axis=0, tiled=True)  72.8 us
    all_to_all x1, waiting for transfers between devices, local(): lax.all_to_all(cleaned, 'tm', split_axis=0, concat_axis=1, tiled=True)  55.1 us
    psum x3, blocking collectives, local(): squares = lax.psum(jnp.dot(gains * gains, onehot, precision=highest), 'det')  36.8 us
    dot_general x3, matrix products, local(): per_det = jnp.dot(onehot, template, precision=highest)  21.6 us
    psum x3, blocking collectives, local(): lax.psum((jnp.sum(masked * per_det, axis=1), jnp.sum(mask * per_det * per...  20 us
    dot_general x1, matrix products, filter_rows(): first_im = -jnp.einsum('kp,rpq->rkq', sin_p, signal, precision=highest)  17.2 us
    dot_general x3, matrix products, local(): jnp.dot(onehot.T, masked * normed[:, None], precision=highest)  16.9 us
  transfers between devices with their start and end apart: 4, of which 4 were waited for; matrix products, arithmetic and copies ran while one was open for 2% of the time, Pallas kernels for 0%

commit v1 on v0

v1 whole, which is shorter than its diff:
```python
import functools
import math

import jax
import jax.numpy as jnp
import numpy as np
from jax import lax
from jax.experimental import pallas as pl
from jax.experimental.pallas import tpu as pltpu
from jax.sharding import PartitionSpec as P

ITERS = 3
Q = 250
QP = 256
GP = 16
CHUNK = 8
MESH = pl.DeviceIdType.MESH
F32 = jnp.float32
BF16 = jnp.bfloat16
NT_DIMS = (((1,), (1,)), ((), ()))


def dot(a, b):
    return jnp.dot(a, b, preferred_element_type=F32)


def dot_nt(a, b):
    return lax.dot_general(a, b, NT_DIMS, preferred_element_type=F32)


def split(a):
    hi = a.astype(BF16)
    return hi, (a - hi.astype(F32)).astype(BF16)


def np_split(a):
    hi = a.astype(BF16)
    return hi, (a - hi.astype(np.float64)).astype(BF16)


def fit_kernel(nd, nt, slabs, own, cyc, rows,
               x_hbm, v_ref, vrc_ref, group_ref, guess_ref, e_ref,
               raw_ref, vraw_ref, tmpl_ref, gains_ref,
               xv, xh, xl, part, small, rbuf, rsmall, tbuf, red,
               load_sem, loc_sem, raw_s, raw_r, val_s, val_r, ps, pr, ss, sr, ts, tr, gs, gr, fs, fr):
    det = lax.axis_index("det")
    tm = lax.axis_index("tm")
    cycles = slabs // cyc
    share = rows // nt * slabs
    vshare = rows // nt * cycles

    def det_peer(off):
        return lax.rem(det + off, nd)

    def tm_peer(off):
        return lax.rem(tm + off, nt)

    loads = [pltpu.make_async_copy(x_hbm.at[:, pl.ds(128 * h, 128)], xv.at[h], load_sem.at[h])
             for h in range(QP // 128)]
    for load in loads:
        load.start()
    barrier = pltpu.get_barrier_semaphore()
    for off in range(1, nd):
        pl.semaphore_signal(barrier, inc=1, device_id=(det_peer(off), tm), device_id_type=MESH)
    for off in range(1, nt):
        pl.semaphore_signal(barrier, inc=1, device_id=(det, tm_peer(off)), device_id_type=MESH)
    pl.semaphore_wait(barrier, nd + nt - 2)

    waits = []
    for off in range(1, nt):
        peer = tm_peer(off)
        copy = pltpu.make_async_remote_copy(
            src_ref=x_hbm.at[pl.ds(peer * share, share)], dst_ref=raw_ref.at[tm],
            send_sem=raw_s.at[off], recv_sem=raw_r.at[off],
            device_id=(det, peer), device_id_type=MESH)
        copy.start()
        waits.append(copy)
        copy = pltpu.make_async_remote_copy(
            src_ref=vrc_ref.at[pl.ds(peer * vshare, vshare)], dst_ref=vraw_ref.at[tm],
            send_sem=val_s.at[off], recv_sem=val_r.at[off],
            device_id=(det, peer), device_id_type=MESH)
        copy.start()
        waits.append(copy)
    own_raw = pltpu.make_async_copy(x_hbm.at[pl.ds(tm * share, share)], raw_ref.at[tm], loc_sem.at[1])
    own_raw.start()
    own_val = pltpu.make_async_copy(vrc_ref.at[pl.ds(tm * vshare, vshare)], vraw_ref.at[tm], loc_sem.at[2])
    own_val.start()
    for load in loads:
        load.wait()

    def prepare(i, carry):
        spread = e_ref[i]
        for c in range(cycles):
            slab = c * cyc + i
            mask = dot(v_ref[c], spread)
            x = jnp.concatenate(
                [xv[h, pl.ds(slab, rows, stride=slabs), :] for h in range(QP // 128)], axis=1)
            hi, lo = split(mask * x)
            xh[slab] = hi
            xl[slab] = lo
        return carry

    lax.fori_loop(0, cyc, prepare, 0)

    hot = (lax.broadcasted_iota(jnp.int32, (GP, rows), 0) == group_ref[...]).astype(F32)
    lane = lax.broadcasted_iota(jnp.int32, (GP, 128), 1)
    gains = guess_ref[...]
    padded = own * nd
    for it in range(ITERS):
        weight = hot * gains
        wh, wl = split(weight)
        wboth = jnp.concatenate([wh, wl], axis=0)
        power = hot * (gains * gains)
        ph, plo = split(power)
        squares = jnp.sum(power, axis=1, keepdims=True)
        counts = jnp.sum(hot, axis=1, keepdims=True)
        for c in range(cycles):
            block_sum = dot(ph, v_ref[c]) + dot(plo, v_ref[c])
            small[it, c] = jnp.where(lane == 64, squares, jnp.where(lane == 65, counts, block_sum))

        copies = []
        for off in range(1, nd):
            copy = pltpu.make_async_remote_copy(
                src_ref=small.at[it], dst_ref=rsmall.at[it, off],
                send_sem=ss.at[it, off], recv_sem=sr.at[it, off],
                device_id=(det_peer(off), tm), device_id_type=MESH)
            copy.start()
            copies.append(copy)

        def weigh(owner):
            def one(k, carry):
                slab = jnp.minimum(owner * own + k, slabs - 1)
                both = dot(wboth, xh[slab])
                part[it, owner * own + k] = both[:GP] + both[GP:] + dot(wh, xl[slab])
                return carry
            lax.fori_loop(0, own, one, 0, unroll=True)

        for off in range(1, nd):
            peer = det_peer(off)
            weigh(peer)
            copy = pltpu.make_async_remote_copy(
                src_ref=part.at[it, pl.ds(peer * own, own)], dst_ref=rbuf.at[it, off],
                send_sem=ps.at[it, off], recv_sem=pr.at[it, off],
                device_id=(peer, tm), device_id_type=MESH)
            copy.start()
            copies.append(copy)
        weigh(det)
        for copy in copies:
            copy.wait_recv()
        waits_send = copies

        first = small[it]
        for off in range(1, nd):
            first = first + rsmall[it, off]
        scale = jnp.sqrt(first[0][:, 64:65] / jnp.maximum(first[0][:, 65:66], 1.0) + 1e-05)
        small[ITERS] = first
        for k in range(own):
            slab = det * own + k
            total = part[it, slab]
            for off in range(1, nd):
                total = total + rbuf[it, off, k]
            safe = jnp.minimum(slab, slabs - 1)
            sums = small[ITERS, lax.div(safe, cyc)]
            sums = jnp.where(lane < 64, sums, 0.0)
            s1, s2 = split(sums)
            spread = e_ref[lax.rem(safe, cyc)]
            wide = dot(s1, spread) + dot(s2, spread)
            tbuf[it, slab] = (total / scale) / (1.0 + wide / (scale * scale))
        gather = []
        for off in range(1, nd):
            copy = pltpu.make_async_remote_copy(
                src_ref=tbuf.at[it, pl.ds(det * own, own)], dst_ref=tbuf.at[it, pl.ds(det * own, own)],
                send_sem=ts.at[it, off], recv_sem=tr.at[it, off],
                device_id=(det_peer(off), tm), device_id_type=MESH)
            copy.start()
            gather.append(copy)
        for off in range(1, nd):
            source = lax.rem(det + nd - off, nd)
            pltpu.make_async_remote_copy(
                src_ref=tbuf.at[it, pl.ds(source * own, own)], dst_ref=tbuf.at[it, pl.ds(source * own, own)],
                send_sem=ts.at[it, off], recv_sem=tr.at[it, off],
                device_id=(det_peer(off), tm), device_id_type=MESH).wait_recv()
        waits_send = waits_send + gather

        if it == ITERS - 1:
            for off in range(1, nt):
                copy = pltpu.make_async_remote_copy(
                    src_ref=tbuf.at[it, pl.ds(0, slabs)], dst_ref=tmpl_ref.at[tm],
                    send_sem=fs.at[off], recv_sem=fr.at[off],
                    device_id=(det, tm_peer(off)), device_id_type=MESH)
                copy.start()
                waits.append(copy)
            own_tmpl = pltpu.make_async_copy(tbuf.at[it, pl.ds(0, slabs)], tmpl_ref.at[tm], loc_sem.at[3])
            own_tmpl.start()

        def correlate(i, carry):
            inner, blocks = carry
            new_blocks = []
            for c in range(cycles):
                slab = c * cyc + i
                th, tl = split(tbuf[it, slab])
                both = dot_nt(jnp.concatenate([th, tl], axis=0), xh[slab])
                inner = inner + both[:GP] + both[GP:] + dot_nt(th, xl[slab])
                sh, sl = split(tbuf[it, slab] * tbuf[it, slab])
                both = dot_nt(jnp.concatenate([sh, sl], axis=0), e_ref[i])
                new_blocks.append(blocks[c] + both[:GP] + both[GP:])
            return inner, tuple(new_blocks)

        inner, blocks = lax.fori_loop(
            0, cyc, correlate,
            (jnp.zeros((GP, rows), F32), tuple(jnp.zeros((GP, 128), F32) for _ in range(cycles))))
        norm = jnp.zeros((GP, rows), F32)
        for c in range(cycles):
            bh, bl = split(blocks[c])
            norm = norm + dot_nt(bh, v_ref[c]) + dot_nt(bl, v_ref[c])
        numer = jnp.sum(hot * inner, axis=0, keepdims=True)
        denom = jnp.sum(hot * norm, axis=0, keepdims=True)
        red[it, tm] = jnp.concatenate([numer, denom, jnp.zeros((6, rows), F32)], axis=0)
        copies = []
        for off in range(1, nt):
            copy = pltpu.make_async_remote_copy(
                src_ref=red.at[it, tm], dst_ref=red.at[it, tm],
                send_sem=gs.at[it, off], recv_sem=gr.at[it, off],
                device_id=(det, tm_peer(off)), device_id_type=MESH)
            copy.start()
            copies.append(copy)
        for off in range(1, nt):
            source = lax.rem(tm + nt - off, nt)
            pltpu.make_async_remote_copy(
                src_ref=red.at[it, source], dst_ref=red.at[it, source],
                send_sem=gs.at[it, off], recv_sem=gr.at[it, off],
                device_id=(det, tm_peer(off)), device_id_type=MESH).wait_recv()
        total = red[it, 0]
        for t in range(1, nt):
            total = total + red[it, t]
        gains = total[0:1] / (1.0 + total[1:2])
        for copy in waits_send + copies:
            copy.wait_send()

    gains_ref[...] = gains
    own_raw.wait()
    own_val.wait()
    own_tmpl.wait()
    for copy in waits:
        copy.wait()


def filter_kernel(nt, slabs, cyc, count, half,
                  group_ref, gain_ref, raw_ref, v_ref, tmpl_ref, w_ref, e_ref,
                  f1_ref, tw_ref, m2_ref, m3_ref, f4_ref,
                  out_ref, mask, stage, spec, ybuf, loc_sem, send, recv):
    det = lax.axis_index("det")
    tm = lax.axis_index("tm")
    total = slabs * nt
    span = CHUNK * slabs
    chunks = count // CHUNK
    cycles = slabs // cyc

    barrier = pltpu.get_barrier_semaphore()
    for off in range(1, nt):
        pl.semaphore_signal(barrier, inc=1, device_id=(det, lax.rem(tm + off, nt)), device_id_type=MESH)
    pl.semaphore_wait(barrier, nt - 1)

    def spread(i, carry):
        for t in range(nt):
            wide = dot(v_ref[t].astype(BF16), e_ref[i])
            for h in range(QP // 128):
                mask[t, h, pl.ds(i, count * cycles, stride=cyc), :] = wide[:, 128 * h:128 * (h + 1)]
        return carry

    lax.fori_loop(0, cyc, spread, 0)

    def remote(chunk, off):
        peer = lax.rem(tm + off, nt)
        return pltpu.make_async_remote_copy(
            src_ref=ybuf.at[peer, pl.ds(chunk * span, span)],
            dst_ref=out_ref.at[pl.ds((tm * chunks + chunk) * span, span)],
            send_sem=send.at[chunk, off], recv_sem=recv.at[chunk, off],
            device_id=(det, peer), device_id_type=MESH)

    def local(chunk):
        return pltpu.make_async_copy(
            ybuf.at[tm, pl.ds(chunk * span, span)],
            out_ref.at[pl.ds((tm * chunks + chunk) * span, span)], loc_sem.at[chunk])

    def three(a, b):
        hi, lo = split(a)
        return dot(hi, b[0]) + dot(lo, b[0]) + dot(hi, b[1])

    def rows_of(read, chunk, k):
        if slabs % 8 == 0:
            return read(pl.ds((chunk * CHUNK + k) * slabs, slabs))
        return read(pl.ds(chunk * span, span))[k * slabs:(k + 1) * slabs]

    def work(chunk, carry):
        for k in range(CHUNK):
            row = chunk * CHUNK + k
            g = group_ref[row]
            parts = []
            for t in range(nt):
                seen = jnp.concatenate(
                    [rows_of(lambda at: mask[t, h, at, :], chunk, k) for h in range(QP // 128)], axis=1)
                stream = rows_of(lambda at: raw_ref[t, at, :], chunk, k)
                parts.append(seen * (stream - gain_ref[row] * tmpl_ref[g, pl.ds(t * slabs, slabs), :]))
            x = jnp.concatenate(parts, axis=0)
            hi, lo = split(x)
            both = dot(f1_ref[...], hi)
            y = both[:2 * half] + both[2 * half:] + dot(f1_ref[pl.ds(0, 2 * half), :], lo)
            re, im = y[:half], y[half:]
            stage[pl.ds(k * half, half), pl.ds(0, QP)] = re * tw_ref[0] + im * tw_ref[1]
            stage[pl.ds(k * half, half), pl.ds(QP, QP)] = im * tw_ref[0] - re * tw_ref[1]
        spec[...] = three(stage[...], m2_ref)
        for k in range(CHUNK):
            w = w_ref[group_ref[chunk * CHUNK + k]]
            for h in range(2):
                at = (pl.ds(k * half, half), pl.ds(h * QP, QP))
                spec[at] = spec[at] * w
        stage[...] = three(spec[...], m3_ref)
        held = []
        for k in range(CHUNK):
            row = chunk * CHUNK + k
            re = stage[pl.ds(k * half, half), pl.ds(0, QP)]
            im = stage[pl.ds(k * half, half), pl.ds(QP, QP)]
            v = jnp.concatenate([re * tw_ref[0] - im * tw_ref[1], im * tw_ref[0] + re * tw_ref[1]], axis=0)
            hi, lo = split(v)
            both = dot(f4_ref[...], hi)
            y = both[:total] + both[total:] + dot(f4_ref[pl.ds(0, total), :], lo)
            held.append(y)
            if slabs % 8 == 0:
                for t in range(nt):
                    ybuf[t, pl.ds(row * slabs, slabs), :] = y[t * slabs:(t + 1) * slabs]
        if slabs % 8:
            for t in range(nt):
                ybuf[t, pl.ds(chunk * span, span), :] = jnp.concatenate(
                    [y[t * slabs:(t + 1) * slabs] for y in held], axis=0)
        for off in range(1, nt):
            remote(chunk, off).start()
        local(chunk).start()
        return carry

    lax.fori_loop(0, chunks, work, 0)

    def finish(chunk, carry):
        local(chunk).wait()
        for off in range(1, nt):
            remote(chunk, off).wait_send()
        for off in range(1, nt):
            source = lax.rem(tm + nt - off, nt)
            pltpu.make_async_remote_copy(
                src_ref=ybuf.at[source, pl.ds(chunk * span, span)],
                dst_ref=out_ref.at[pl.ds((source * chunks + chunk) * span, span)],
                send_sem=send.at[chunk, off], recv_sem=recv.at[chunk, off],
                device_id=(det, source), device_id_type=MESH).wait_recv()
        return carry

    lax.fori_loop(0, chunks, finish, 0)


def constants(total):
    length = total * Q
    half = -(-(total // 2 + 1) // 8) * 8
    kp = np.arange(total // 2 + 1)
    n = kp.size
    p = np.arange(total)
    angle = 2 * np.pi / total * (kp[:, None] * p[None, :] % total)
    f1 = np.zeros((2 * half, total))
    f1[:n] = np.cos(angle)
    f1[half:half + n] = -np.sin(angle)
    hi, lo = np_split(f1)
    f1 = np.concatenate([hi, lo], axis=0)
    twice = np.where((kp == 0) | (2 * kp == total), 1.0, 2.0) / length
    f4 = np.zeros((total, 2 * half))
    f4[:, :n] = (np.cos(angle) * twice[:, None]).T
    f4[:, half:half + n] = -(np.sin(angle) * twice[:, None]).T
    hi, lo = np_split(f4)
    f4 = np.concatenate([hi, lo], axis=0)
    q = np.arange(Q)
    angle = 2 * np.pi / length * (kp[:, None] * q[None, :])
    tw = np.zeros((2, half, QP), np.float32)
    tw[0, :n, :Q] = np.cos(angle)
    tw[1, :n, :Q] = np.sin(angle)
    angle = 2 * np.pi / Q * (q[:, None] * q[None, :] % Q)
    c, s = np.cos(angle), np.sin(angle)

    def complex_table(sign):
        m = np.zeros((2 * QP, 2 * QP))
        m[:Q, :Q] = c
        m[QP:QP + Q, :Q] = -sign * s
        m[:Q, QP:QP + Q] = sign * s
        m[QP:QP + Q, QP:QP + Q] = c
        return np.stack(np_split(m))

    return half, n, f1, f4, tw, complex_table(-1.0), complex_table(1.0)


def local(timestreams, wafer_group, valid_blocks, gain_guess, inverse_psd):
    nd, nt = lax.axis_size("det"), lax.axis_size("tm")
    rows, samp = timestreams.shape
    groups = inverse_psd.shape[0]
    block = samp // valid_blocks.shape[1]
    cyc = block // math.gcd(block, Q)
    per = cyc * Q // block
    slabs = samp // Q
    cycles = slabs // cyc
    own = -(-slabs // nd)
    padded = own * nd
    count = rows // nt
    total = slabs * nt
    half, n, f1, f4, tw, m2, m3 = constants(total)
    spread = np.zeros((cyc, 128, QP), np.float32)
    for i in range(cyc):
        spread[i, (i * Q + np.arange(Q)) // block, np.arange(Q)] = 1.0
    e = jnp.asarray(spread.astype(BF16))

    x2 = jnp.pad(timestreams.reshape(rows, slabs, Q), ((0, 0), (0, 0), (0, QP - Q))).reshape(rows * slabs, QP)
    vrc = jnp.pad(valid_blocks.astype(F32).reshape(rows, cycles, per), ((0, 0), (0, 0), (0, 128 - per)))
    v = jnp.transpose(vrc, (1, 0, 2)).astype(BF16)
    vrc = vrc.reshape(rows * cycles, 128)

    vmem = pl.BlockSpec(memory_space=pltpu.VMEM)
    hbm = pl.BlockSpec(memory_space=pl.ANY)
    smem = pl.BlockSpec(memory_space=pltpu.SMEM)
    dma = pltpu.SemaphoreType.DMA
    raw, vraw, tmpl, gains = pl.pallas_call(
        functools.partial(fit_kernel, nd, nt, slabs, own, cyc, rows),
        out_shape=(
            jax.ShapeDtypeStruct((nt, count * slabs, QP), F32),
            jax.ShapeDtypeStruct((nt, count * cycles, 128), F32),
            jax.ShapeDtypeStruct((nt, slabs, GP, QP), F32),
            jax.ShapeDtypeStruct((1, rows), F32),
        ),
        in_specs=[hbm, vmem, vmem, vmem, vmem, vmem],
        out_specs=(hbm, vmem, hbm, vmem),
        scratch_shapes=[
            pltpu.VMEM((QP // 128, rows * slabs, 128), F32),
            pltpu.VMEM((slabs, rows, QP), BF16),
            pltpu.VMEM((slabs, rows, QP), BF16),
            pltpu.VMEM((ITERS, padded, GP, QP), F32),
            pltpu.VMEM((ITERS + 1, cycles, GP, 128), F32),
            pltpu.VMEM((ITERS, nd, own, GP, QP), F32),
            pltpu.VMEM((ITERS, nd, cycles, GP, 128), F32),
            pltpu.VMEM((ITERS, padded, GP, QP), F32),
            pltpu.VMEM((ITERS, nt, 8, rows), F32),
            dma((QP // 128,)), dma((4,)), dma((nt,)), dma((nt,)), dma((nt,)), dma((nt,)),
            dma((ITERS, nd)), dma((ITERS, nd)), dma((ITERS, nd)), dma((ITERS, nd)),
            dma((ITERS, nd)), dma((ITERS, nd)), dma((ITERS, nt)), dma((ITERS, nt)),
            dma((nt,)), dma((nt,)),
        ],
        compiler_params=pltpu.CompilerParams(
            collective_id=0, has_side_effects=True, vmem_limit_bytes=50 * 2**20),
        name="fit",
    )(x2, v, vrc, wafer_group.reshape(1, rows), gain_guess.reshape(1, rows), e)

    gains = gains.reshape(rows)
    mine = lax.axis_index("tm")
    template = lax.dynamic_index_in_dim(tmpl, mine, 0, False)[:, :groups, :Q]
    template = jnp.transpose(template, (1, 0, 2)).reshape(groups, samp)
    by_group = jnp.transpose(tmpl.reshape(total, GP, QP), (1, 0, 2))[:groups]
    even = 0.5 * (inverse_psd + jnp.roll(jnp.flip(inverse_psd, 1), 1, axis=1))
    weights = jnp.transpose(even.reshape(groups, Q, total)[:, :, :n], (0, 2, 1))
    weights = jnp.pad(weights, ((0, 0), (0, half - n), (0, QP - Q)))
    my_group = lax.dynamic_slice_in_dim(wafer_group, mine * count, count)
    my_gains = lax.dynamic_slice_in_dim(gains, mine * count, count)

    out = pl.pallas_call(
        functools.partial(filter_kernel, nt, slabs, cyc, count, half),
        out_shape=jax.ShapeDtypeStruct((rows * slabs, QP), F32),
        in_specs=[smem, smem] + [vmem] * 10,
        out_specs=hbm,
        scratch_shapes=[
            pltpu.VMEM((nt, QP // 128, count * slabs, 128), F32),
            pltpu.VMEM((CHUNK * half, 2 * QP), F32),
            pltpu.VMEM((CHUNK * half, 2 * QP), F32),
            pltpu.VMEM((nt, count * slabs, QP), F32),
            dma((count // CHUNK,)), dma((count // CHUNK, nt)), dma((count // CHUNK, nt)),
        ],
        compiler_params=pltpu.CompilerParams(
            collective_id=1, has_side_effects=True, vmem_limit_bytes=50 * 2**20),
        name="filter",
    )(my_group, my_gains, raw, vraw, by_group, weights, e,
      jnp.asarray(f1), jnp.asarray(tw), jnp.asarray(m2), jnp.asarray(m3), jnp.asarray(f4))
    filtered = out.reshape(rows, slabs, QP)[:, :, :Q].reshape(rows, samp)
    return (filtered, gains, template)


def solution(mesh):
    in_specs = (P("det", "tm"), P("det"), P("det", "tm"), P("det"), P())
    out_specs = (P("det", "tm"), P("det"), P(None, "tm"))
    return jax.shard_map(local, mesh=mesh, in_specs=in_specs, out_specs=out_specs, check_vma=False)
```

time: 739 us -> 370 us (0.50)
  waiting for transfers between devices: 293 us -> 0 us
  Pallas kernels: 0 us -> 228 us
  matrix products: 206 us -> 0 us
  blocking collectives: 130 us -> 0 us
  local copies, waits for them, and re-layouts: 61.3 us -> 132 us
  other arithmetic: 17.3 us -> 2.42 us
  between operations: 14.1 us -> 0.8 us
    psum x3 -> x0, waiting for transfers between devices: 237 us -> none  [local(): lax.psum((jnp.dot(onehot.T, masked * normed[:, None], precision=highest),...]
    pallas_call x0 -> x2, Pallas kernels: none -> 228 us  [the longest x1 149 us: local(): pl.pallas_call(functools.partial(fit_kernel, nd, nt, slabs, own, cyc, row...]
    dot_general x28 -> x0, matrix products: 206 us -> none  [the longest x3 21.6 us: local(): per_det = jnp.dot(onehot, template, precision=highest)]
    unnamed x23 -> x24, local copies, waits for them, and re-layouts: 6.57 us -> 96.5 us
    all_to_all x1 -> x0, blocking collectives: 72.8 us -> none  [local(): lax.all_to_all(filtered_rows, 'tm', split_axis=1, concat_axis=0, tiled=True)]
    psum x6 -> x0, blocking collectives: 56.8 us -> none  [the longest x3 36.8 us: local(): squares = lax.psum(jnp.dot(gains * gains, onehot, precision=highest), 'det')]
    all_to_all x1 -> x0, waiting for transfers between devices: 55.1 us -> none  [local(): lax.all_to_all(cleaned, 'tm', split_axis=0, concat_axis=1, tiled=True)]
    all_to_all x3 -> x0, local copies, waits for them, and re-layouts: 22.2 us -> none  [the longest x2 12.9 us: local(): lax.all_to_all(filtered_rows, 'tm', split_axis=1, concat_axis=0, tiled=True)]
  transfers between devices with their start and end apart: 4 -> 0, of which waited for: 4 -> 0; matrix products, arithmetic and copies ran while one was open for 2% -> 0% of each run, Pallas kernels for 0% -> 0%
where the time goes in v1:
time: 370 us; the launch traced here: 363 us
  Pallas kernels  228 us (62%)
  local copies, waits for them, and re-layouts  132 us (36%)
    pallas_call x1, Pallas kernels, local(): pl.pallas_call(functools.partial(fit_kernel, nd, nt, slabs, own, cyc, row...  149 us
    unnamed x24, local copies, waits for them, and re-layouts  96.5 us
    pallas_call x1, Pallas kernels, local(): pl.pallas_call(functools.partial(filter_kernel, nt, slabs, cyc, count, ha...  79 us
    reshape x2, local copies, waits for them, and re-layouts, local(): filtered = out.reshape(rows, slabs, QP)[:, :, :Q].reshape(rows, samp)  14.6 us

profile of v1, /device:TPU:13, one launch (start us, length us, event | category | flops | bytes accessed | tf_op | source)
XLA Modules:
  0.0 362.8 jit_solution(10859893704345577057)
XLA Ops:
  0.6 0.0 copy-start.8
  0.6 0.9 dynamic_slice.12.group_ref
  1.5 0.8 convert_element_type.14
  2.4 0.1 copy.25
  2.5 0.2 copy.35
  2.7 0.1 pad.13.clone
  2.8 0.0 copy-done.8
  2.9 1.6 slice.26
  4.4 85.9 %reverse.2 = f32[12,24064]{1,0:T(8,128)} reverse(f32[12,24064]{1,0:T(8,128)} %bitcast.32), dimensions={1} | reverse | bytes 2310144
  90.4 0.0 slice-start
  90.4 1.9 slice.36
  92.2 0.0 slice-done
  92.3 1.6 fusion
  93.9 2.1 reshape.50
  95.9 0.5 copy.31
  96.4 0.1 pad.14.w_ref
  96.5 6.6 %reshape.43 = f32[256,24,250]{0,2,1:T(8,128)} reshape(f32[256,6000]{0,1:T(8,128)} %param.11) | data formatting | bytes 12288000 | tf_op jit(solution)/shard_map/reshape | solution.py:415
  103.1 6.7 %copy.33 = f32[256,24,250]{2,1,0:T(8,128)} copy(f32[256,24,250]{0,2,1:T(8,128)} %reshape.43) | data formatting | bytes 12288000
  109.7 0.0 copy-start
  109.7 0.0 copy-start.6
  109.7 0.0 copy-start.7
  109.7 5.9 %pad.12.clone = f32[256,24,256]{2,1,0:T(8,128)} pad(f32[256,24,250]{2,1,0:T(8,128)} %copy.33, f32[]{:T(128)} %constant.29.clone.1), padding=0_0x0_0x0_6 | pad | bytes 12435460 | tf_op jit(solution)/shard_map/jit(_pad)/pad | solution.py:415
  115.6 0.0 copy-done
  115.6 0.0 copy-done.6
  115.7 0.0 copy-done.7
  115.7 148.7 %fit.1 = (f32[4,1536,256]{2,1,0:T(8,128)}, f32[4,128,128]{2,1,0:T(8,128)S(1)}, f32[4,24,16,256]{3,2,1,0:T(8,128)S(1)}, f32[1,256]{1,0:T(1,128)S(1)}) custom-call(f32[6144,256]{1,0:T(8,128)} %bitcast.30, bf16[2,256,128]{2,1,0:T(8,128)(2,1)S(1)} %convert_bitcast_fusion.v_ref, f32[512,128]{1,0:T(8,128)S(1)} %bitcast.25, s32[1,256]{1,0:T(1,128)S(1)} %bitcast.26, ...), custom_call_target="tpu_custom_call" | custom-call | tf_op jit(solution)/shard_map/fit/pallas_call | solution.py:424
  264.4 0.1 dynamic-slice_bitcast_fusion.1.gain_ref
  264.5 0.9 copy.27
  265.4 0.0 copy-start.1
  265.4 0.0 copy-start.2
  265.4 0.0 copy-start.3
  265.5 0.0 copy-start.4
  265.5 0.0 copy-start.5
  265.5 1.1 slice.31.tmpl_ref
  266.6 0.3 copy-done.1
  266.9 0.5 copy-done.2
  267.4 0.0 copy-done.3
  267.4 0.0 copy-done.4
  267.4 0.0 copy-done.5
  267.4 79.0 %filter.1 = f32[6144,256]{1,0:T(8,128)} custom-call(s32[64]{0:T(128)S(1)} %dynamic_slice.12.group_ref, f32[64]{0:T(128)S(1)} %dynamic-slice_bitcast_fusion.1.gain_ref, f32[4,1536,256]{2,1,0:T(8,128)} %get-tuple-element.8.raw_ref, f32[4,128,128]{2,1,0:T(8,128)S(1)} %get-tuple-element.9.v_ref, f32[12,96,256]{2,1,0:T(8,128)} %slice.31.tmpl_ref, ...), custom_call_target="tpu_custom_call" | custom-call | tf_op jit(solution)/shard_map/filter/pallas_call | solution.py:465
  346.4 8.1 %reshape.55 = f32[256,6000]{1,0:T(8,128)} reshape(f32[256,24,250]{2,1,0:T(8,128)} %bitcast.29) | data formatting | bytes 12288000 | tf_op jit(solution)/shard_map/reshape | solution.py:482
  354.5 6.5 %copy.34 = f32[256,6000]{0,1:T(8,128)} copy(f32[256,6000]{1,0:T(8,128)} %reshape.55) | data formatting | bytes 12288000 | tf_op jit(solution)/shard_map/reshape | solution.py:482
  361.1 0.2 copy.30
  361.3 1.0 reshape.54
  362.2 0.6 copy.37
  (4 shorter events, 0.1 us)
Async XLA Ops:
  0.6 2.2 copy-start.8
  90.4 1.9 slice-start
  109.7 5.9 %copy-start = (bf16[12,128,256]{2,1,0:T(8,128)(2,1)S(1)}, bf16[12,128,256]{2,1,0:T(8,128)(2,1)}, u32[]{:S(2)}) copy-start(bf16[12,128,256]{2,1,0:T(8,128)(2,1)} %constant.32.clone.e_ref) | copy-start | bytes 2359300
  109.7 5.9 %copy-start.6 = (s32[256]{0:T(256)S(1)}, s32[256]{0:T(256)}, u32[]{:S(2)}) copy-start(s32[256]{0:T(256)} %param.12) | copy-start | bytes 3076
  109.7 5.9 %copy-start.7 = (f32[256]{0:T(256)S(1)}, f32[256]{0:T(256)}, u32[]{:S(2)}) copy-start(f32[256]{0:T(256)} %param.14) | copy-start | bytes 3076
  265.4 1.5 copy-start.1
  265.4 2.0 copy-start.2
  265.4 1.9 copy-start.3
  265.5 1.9 copy-start.4
  265.5 1.9 copy-start.5

commit v2 on v1

--- a/solution.py
+++ b/solution.py
@@ -13,6 +13,8 @@
 Q = 250
 QP = 256
 GP = 16
+HALVES = QP // 128
+BAND = 32
 CHUNK = 8
 MESH = pl.DeviceIdType.MESH
 F32 = jnp.float32
@@ -38,11 +40,25 @@
     return hi, (a - hi.astype(np.float64)).astype(BF16)
 
 
+def pack_kernel(slabs, x_ref, out_ref):
+    for p in range(slabs):
+        wide = x_ref[:, Q * p:Q * (p + 1)]
+        wide = jnp.concatenate([wide, jnp.zeros((BAND, QP - Q), F32)], axis=1)
+        for h in range(HALVES):
+            out_ref[h, pl.ds(p, BAND, stride=slabs), :] = wide[:, 128 * h:128 * (h + 1)]
+
+
+def unpack_kernel(slabs, y_ref, out_ref):
+    for p in range(slabs):
+        wide = jnp.concatenate([y_ref[h, pl.ds(p, BAND, stride=slabs), :] for h in range(HALVES)], axis=1)
+        out_ref[:, Q * p:Q * (p + 1)] = wide[:, :Q]
+
+
 def fit_kernel(nd, nt, slabs, own, cyc, rows,
                x_hbm, v_ref, vrc_ref, group_ref, guess_ref, e_ref,
                raw_ref, vraw_ref, tmpl_ref, gains_ref,
                xv, xh, xl, part, small, rbuf, rsmall, tbuf, red,
-               load_sem, loc_sem, raw_s, raw_r, val_s, val_r, ps, pr, ss, sr, ts, tr, gs, gr, fs, fr):
+               loc_sem, raw_s, raw_r, val_s, val_r, ps, pr, ss, sr, ts, tr, gs, gr, fs, fr):
     det = lax.axis_index("det")
     tm = lax.axis_index("tm")
     cycles = slabs // cyc
@@ -55,10 +71,8 @@
     def tm_peer(off):
         return lax.rem(tm + off, nt)
 
-    loads = [pltpu.make_async_copy(x_hbm.at[:, pl.ds(128 * h, 128)], xv.at[h], load_sem.at[h])
-             for h in range(QP // 128)]
-    for load in loads:
-        load.start()
+    load = pltpu.make_async_copy(x_hbm, xv, loc_sem.at[0])
+    load.start()
     barrier = pltpu.get_barrier_semaphore()
     for off in range(1, nd):
         pl.semaphore_signal(barrier, inc=1, device_id=(det_peer(off), tm), device_id_type=MESH)
@@ -70,7 +84,7 @@
     for off in range(1, nt):
         peer = tm_peer(off)
         copy = pltpu.make_async_remote_copy(
-            src_ref=x_hbm.at[pl.ds(peer * share, share)], dst_ref=raw_ref.at[tm],
+            src_ref=x_hbm.at[:, pl.ds(peer * share, share)], dst_ref=raw_ref.at[tm],
             send_sem=raw_s.at[off], recv_sem=raw_r.at[off],
             device_id=(det, peer), device_id_type=MESH)
         copy.start()
@@ -81,12 +95,11 @@
             device_id=(det, peer), device_id_type=MESH)
         copy.start()
         waits.append(copy)
-    own_raw = pltpu.make_async_copy(x_hbm.at[pl.ds(tm * share, share)], raw_ref.at[tm], loc_sem.at[1])
+    own_raw = pltpu.make_async_copy(x_hbm.at[:, pl.ds(tm * share, share)], raw_ref.at[tm], loc_sem.at[1])
     own_raw.start()
     own_val = pltpu.make_async_copy(vrc_ref.at[pl.ds(tm * vshare, vshare)], vraw_ref.at[tm], loc_sem.at[2])
     own_val.start()
-    for load in loads:
-        load.wait()
+    load.wait()
 
     def prepare(i, carry):
         spread = e_ref[i]
@@ -94,7 +107,7 @@
             slab = c * cyc + i
             mask = dot(v_ref[c], spread)
             x = jnp.concatenate(
-                [xv[h, pl.ds(slab, rows, stride=slabs), :] for h in range(QP // 128)], axis=1)
+                [xv[h, pl.ds(slab, rows, stride=slabs), :] for h in range(HALVES)], axis=1)
             hi, lo = split(mask * x)
             xh[slab] = hi
             xl[slab] = lo
@@ -264,7 +277,7 @@
     def spread(i, carry):
         for t in range(nt):
             wide = dot(v_ref[t].astype(BF16), e_ref[i])
-            for h in range(QP // 128):
+            for h in range(HALVES):
                 mask[t, h, pl.ds(i, count * cycles, stride=cyc), :] = wide[:, 128 * h:128 * (h + 1)]
         return carry
 
@@ -273,15 +286,15 @@
     def remote(chunk, off):
         peer = lax.rem(tm + off, nt)
         return pltpu.make_async_remote_copy(
-            src_ref=ybuf.at[peer, pl.ds(chunk * span, span)],
-            dst_ref=out_ref.at[pl.ds((tm * chunks + chunk) * span, span)],
+            src_ref=ybuf.at[peer, :, pl.ds(chunk * span, span)],
+            dst_ref=out_ref.at[:, pl.ds((tm * chunks + chunk) * span, span)],
             send_sem=send.at[chunk, off], recv_sem=recv.at[chunk, off],
             device_id=(det, peer), device_id_type=MESH)
 
     def local(chunk):
         return pltpu.make_async_copy(
-            ybuf.at[tm, pl.ds(chunk * span, span)],
-            out_ref.at[pl.ds((tm * chunks + chunk) * span, span)], loc_sem.at[chunk])
+            ybuf.at[tm, :, pl.ds(chunk * span, span)],
+            out_ref.at[:, pl.ds((tm * chunks + chunk) * span, span)], loc_sem.at[chunk])
 
     def three(a, b):
         hi, lo = split(a)
@@ -299,8 +312,9 @@
             parts = []
             for t in range(nt):
                 seen = jnp.concatenate(
-                    [rows_of(lambda at: mask[t, h, at, :], chunk, k) for h in range(QP // 128)], axis=1)
-                stream = rows_of(lambda at: raw_ref[t, at, :], chunk, k)
+                    [rows_of(lambda at: mask[t, h, at, :], chunk, k) for h in range(HALVES)], axis=1)
+                stream = jnp.concatenate(
+                    [rows_of(lambda at: raw_ref[t, h, at, :], chunk, k) for h in range(HALVES)], axis=1)
                 parts.append(seen * (stream - gain_ref[row] * tmpl_ref[g, pl.ds(t * slabs, slabs), :]))
             x = jnp.concatenate(parts, axis=0)
             hi, lo = split(x)
@@ -328,11 +342,13 @@
             held.append(y)
             if slabs % 8 == 0:
                 for t in range(nt):
-                    ybuf[t, pl.ds(row * slabs, slabs), :] = y[t * slabs:(t + 1) * slabs]
+                    for h in range(HALVES):
+                        ybuf[t, h, pl.ds(row * slabs, slabs), :] = y[t * slabs:(t + 1) * slabs, 128 * h:128 * (h + 1)]
         if slabs % 8:
             for t in range(nt):
-                ybuf[t, pl.ds(chunk * span, span), :] = jnp.concatenate(
-                    [y[t * slabs:(t + 1) * slabs] for y in held], axis=0)
+                joined = jnp.concatenate([y[t * slabs:(t + 1) * slabs] for y in held], axis=0)
+                for h in range(HALVES):
+                    ybuf[t, h, pl.ds(chunk * span, span), :] = joined[:, 128 * h:128 * (h + 1)]
         for off in range(1, nt):
             remote(chunk, off).start()
         local(chunk).start()
@@ -347,8 +363,8 @@
         for off in range(1, nt):
             source = lax.rem(tm + nt - off, nt)
             pltpu.make_async_remote_copy(
-                src_ref=ybuf.at[source, pl.ds(chunk * span, span)],
-                dst_ref=out_ref.at[pl.ds((source * chunks + chunk) * span, span)],
+                src_ref=ybuf.at[source, :, pl.ds(chunk * span, span)],
+                dst_ref=out_ref.at[:, pl.ds((source * chunks + chunk) * span, span)],
                 send_sem=send.at[chunk, off], recv_sem=recv.at[chunk, off],
                 device_id=(det, source), device_id_type=MESH).wait_recv()
         return carry
@@ -412,7 +428,15 @@
         spread[i, (i * Q + np.arange(Q)) // block, np.arange(Q)] = 1.0
     e = jnp.asarray(spread.astype(BF16))
 
-    x2 = jnp.pad(timestreams.reshape(rows, slabs, Q), ((0, 0), (0, 0), (0, QP - Q))).reshape(rows * slabs, QP)
+    x2 = pl.pallas_call(
+        functools.partial(pack_kernel, slabs),
+        out_shape=jax.ShapeDtypeStruct((HALVES, rows * slabs, 128), F32),
+        grid=(rows // BAND,),
+        in_specs=[pl.BlockSpec((BAND, samp), lambda i: (i, 0))],
+        out_specs=pl.BlockSpec((HALVES, BAND * slabs, 128), lambda i: (0, i, 0)),
+        compiler_params=pltpu.CompilerParams(vmem_limit_bytes=32 * 2**20),
+        name="pack",
+    )(timestreams)
     vrc = jnp.pad(valid_blocks.astype(F32).reshape(rows, cycles, per), ((0, 0), (0, 0), (0, 128 - per)))
     v = jnp.transpose(vrc, (1, 0, 2)).astype(BF16)
     vrc = vrc.reshape(rows * cycles, 128)
@@ -424,7 +448,7 @@
     raw, vraw, tmpl, gains = pl.pallas_call(
         functools.partial(fit_kernel, nd, nt, slabs, own, cyc, rows),
         out_shape=(
-            jax.ShapeDtypeStruct((nt, count * slabs, QP), F32),
+            jax.ShapeDtypeStruct((nt, HALVES, count * slabs, 128), F32),
             jax.ShapeDtypeStruct((nt, count * cycles, 128), F32),
             jax.ShapeDtypeStruct((nt, slabs, GP, QP), F32),
             jax.ShapeDtypeStruct((1, rows), F32),
@@ -432,7 +456,7 @@
         in_specs=[hbm, vmem, vmem, vmem, vmem, vmem],
         out_specs=(hbm, vmem, hbm, vmem),
         scratch_shapes=[
-            pltpu.VMEM((QP // 128, rows * slabs, 128), F32),
+            pltpu.VMEM((HALVES, rows * slabs, 128), F32),
             pltpu.VMEM((slabs, rows, QP), BF16),
             pltpu.VMEM((slabs, rows, QP), BF16),
             pltpu.VMEM((ITERS, padded, GP, QP), F32),
@@ -441,7 +465,7 @@
             pltpu.VMEM((ITERS, nd, cycles, GP, 128), F32),
             pltpu.VMEM((ITERS, padded, GP, QP), F32),
             pltpu.VMEM((ITERS, nt, 8, rows), F32),
-            dma((QP // 128,)), dma((4,)), dma((nt,)), dma((nt,)), dma((nt,)), dma((nt,)),
+            dma((4,)), dma((nt,)), dma((nt,)), dma((nt,)), dma((nt,)),
             dma((ITERS, nd)), dma((ITERS, nd)), dma((ITERS, nd)), dma((ITERS, nd)),
             dma((ITERS, nd)), dma((ITERS, nd)), dma((ITERS, nt)), dma((ITERS, nt)),
             dma((nt,)), dma((nt,)),
@@ -456,22 +480,30 @@
     template = lax.dynamic_index_in_dim(tmpl, mine, 0, False)[:, :groups, :Q]
     template = jnp.transpose(template, (1, 0, 2)).reshape(groups, samp)
     by_group = jnp.transpose(tmpl.reshape(total, GP, QP), (1, 0, 2))[:groups]
-    even = 0.5 * (inverse_psd + jnp.roll(jnp.flip(inverse_psd, 1), 1, axis=1))
-    weights = jnp.transpose(even.reshape(groups, Q, total)[:, :, :n], (0, 2, 1))
-    weights = jnp.pad(weights, ((0, 0), (0, half - n), (0, QP - Q)))
+    kp = np.arange(n)
+    pick = np.zeros((total, 2 * half), np.float32)
+    pick[kp, kp] = 0.5
+    pick[(total - kp) % total, half + kp] = 0.5
+    both = jnp.einsum("gjp,pk->gkj", inverse_psd.reshape(groups, Q, total), pick, precision=lax.Precision.HIGHEST)
+    flips = np.zeros((2, Q, QP), np.float32)
+    flips[0, (Q - np.arange(Q)) % Q, np.arange(Q)] = 1.0
+    flips[1, Q - 1 - np.arange(Q), np.arange(Q)] = 1.0
+    edge = jnp.dot(both[:, half], flips[0], precision=lax.Precision.HIGHEST)
+    inside = jnp.einsum("gkj,jq->gkq", both[:, half + 1:], flips[1], precision=lax.Precision.HIGHEST)
+    weights = jnp.pad(both[:, :half], ((0, 0), (0, 0), (0, QP - Q))) + jnp.concatenate([edge[:, None], inside], axis=1)
     my_group = lax.dynamic_slice_in_dim(wafer_group, mine * count, count)
     my_gains = lax.dynamic_slice_in_dim(gains, mine * count, count)
 
     out = pl.pallas_call(
         functools.partial(filter_kernel, nt, slabs, cyc, count, half),
-        out_shape=jax.ShapeDtypeStruct((rows * slabs, QP), F32),
+        out_shape=jax.ShapeDtypeStruct((HALVES, rows * slabs, 128), F32),
         in_specs=[smem, smem] + [vmem] * 10,
         out_specs=hbm,
         scratch_shapes=[
-            pltpu.VMEM((nt, QP // 128, count * slabs, 128), F32),
+            pltpu.VMEM((nt, HALVES, count * slabs, 128), F32),
             pltpu.VMEM((CHUNK * half, 2 * QP), F32),
             pltpu.VMEM((CHUNK * half, 2 * QP), F32),
-            pltpu.VMEM((nt, count * slabs, QP), F32),
+            pltpu.VMEM((nt, HALVES, count * slabs, 128), F32),
             dma((count // CHUNK,)), dma((count // CHUNK, nt)), dma((count // CHUNK, nt)),
         ],
         compiler_params=pltpu.CompilerParams(
@@ -479,7 +511,15 @@
         name="filter",
     )(my_group, my_gains, raw, vraw, by_group, weights, e,
       jnp.asarray(f1), jnp.asarray(tw), jnp.asarray(m2), jnp.asarray(m3), jnp.asarray(f4))
-    filtered = out.reshape(rows, slabs, QP)[:, :, :Q].reshape(rows, samp)
+    filtered = pl.pallas_call(
+        functools.partial(unpack_kernel, slabs),
+        out_shape=jax.ShapeDtypeStruct((rows, samp), F32),
+        grid=(rows // BAND,),
+        in_specs=[pl.BlockSpec((HALVES, BAND * slabs, 128), lambda i: (0, i, 0))],
+        out_specs=pl.BlockSpec((BAND, samp), lambda i: (i, 0)),
+        compiler_params=pltpu.CompilerParams(vmem_limit_bytes=32 * 2**20),
+        name="unpack",
+    )(out)
     return (filtered, gains, template)
 
 

time: 370 us -> 271 us (0.73); the launches traced: 363 us -> 270 us
  local copies, waits for them, and re-layouts: 132 us -> 32.1 us
  Pallas kernels: 228 us -> 234 us
    unnamed x24 -> x34, local copies, waits for them, and re-layouts: 96.5 us -> 25.7 us
    reshape x4 -> x1, local copies, waits for them, and re-layouts: 23.3 us -> 2.09 us  [local(): inverse_psd.reshape(groups, Q, total)]
    pad x2 -> x0, local copies, waits for them, and re-layouts: 5.97 us -> none  [the longest x1 5.92 us: local(): jnp.pad(timestreams.reshape(rows, slabs, Q), ((0, 0), (0, 0), (0, QP - Q)))]
    pallas_call x0 -> x2, Pallas kernels: none -> 5.96 us  [the longest x1 3.34 us: local(): pl.pallas_call(functools.partial(pack_kernel, slabs), out_shape=jax.Shape...]
where the time goes in v2:
time: 271 us; the launch traced here: 270 us
  Pallas kernels  234 us (86%)
  local copies, waits for them, and re-layouts  32.1 us (12%)
    pallas_call x1, Pallas kernels, local(): pl.pallas_call(functools.partial(fit_kernel, nd, nt, slabs, own, cyc, row...  149 us
    pallas_call x1, Pallas kernels, local(): pl.pallas_call(functools.partial(filter_kernel, nt, slabs, cyc, count, ha...  79 us
    unnamed x34, local copies, waits for them, and re-layouts  25.7 us

profile of v2, /device:TPU:13, one launch (start us, length us, event | category | flops | bytes accessed | tf_op | source)
XLA Modules:
  0.0 270.1 jit_solution(3321915671557034261)
XLA Ops:
  0.6 0.8 dynamic_slice.12.group_ref
  1.4 0.8 convert_element_type.12
  2.2 0.1 copy.29
  2.4 0.2 copy.39
  2.6 0.1 pad.8.clone
  2.7 0.0 copy-start.14
  2.7 2.1 reshape.36
  4.8 0.0 copy-done.14
  4.8 0.0 copy-start.13
  4.8 0.0 copy-start.12
  4.9 1.5 convolution_bitcast_fusion
  6.4 0.0 copy-done.13
  6.4 0.2 fusion.2
  6.7 0.0 copy-done.12
  6.7 0.7 fusion
  7.5 0.1 maximum_add_fusion.w_ref
  7.6 6.7 %copy.28.x_ref = f32[256,6000]{1,0:T(8,128)} copy(f32[256,6000]{0,1:T(8,128)} %param.14) | data formatting | bytes 12288000 | tf_op args[0]
  14.3 0.0 copy-start.3
  14.3 2.7 %copy-done.3 = f32[256,6000]{1,0:T(8,128)S(1)} copy-done((f32[256,6000]{1,0:T(8,128)S(1)}, f32[256,6000]{1,0:T(8,128)}, u32[]{:S(2)}) %copy-start.3) | copy-done | bytes 6144024
  17.1 0.0 copy-start.4
  17.1 0.0 copy-start.10
  17.1 0.0 copy-start.11
  17.1 3.3 %pack.1.x_hbm = f32[2,6144,128]{2,1,0:T(8,128)S(1)} custom-call(f32[256,6000]{1,0:T(8,128)S(1)} %copy-done.3), custom_call_target="tpu_custom_call" | custom-call | tf_op jit(solution)/shard_map/pack/pallas_call | solution.py:431
  20.4 0.0 copy-start.1
  20.4 2.6 copy-done.1
  23.1 0.0 copy-done.4
  23.1 0.0 copy-done.10
  23.1 0.0 copy-done.11
  23.1 148.7 %fit.1 = (f32[4,2,1536,128]{3,2,1,0:T(8,128)}, f32[4,128,128]{2,1,0:T(8,128)S(1)}, f32[4,24,16,256]{3,2,1,0:T(8,128)S(1)}, f32[1,256]{1,0:T(1,128)S(1)}) custom-call(f32[2,6144,128]{2,1,0:T(8,128)} %copy-done.1, bf16[2,256,128]{2,1,0:T(8,128)(2,1)S(1)} %convert_bitcast_fusion.v_ref, f32[512,128]{1,0:T(8,128)S(1)} %bitcast.28, s32[1,256]{1,0:T(1,128)S(1)} %bitcast.29, ...), custom_call_target="tpu_custom_call" | custom-call | tf_op jit(solution)/shard_map/fit/pallas_call | solution.py:448
  171.8 0.1 dynamic-slice_bitcast_fusion.1.gain_ref
  171.9 0.9 copy.31
  172.8 0.0 copy-start.5
  172.8 0.0 copy-start.6
  172.8 0.0 copy-start.7
  172.8 0.0 copy-start.8
  172.9 0.0 copy-start.9
  172.9 1.1 slice.20.tmpl_ref
  174.0 0.5 copy-done.5
  174.4 0.3 copy-done.6
  174.8 0.0 copy-done.7
  174.8 0.0 copy-done.8
  174.8 0.0 copy-done.9
  174.8 79.0 %filter.1.y_ref = f32[2,6144,128]{2,1,0:T(8,128)} custom-call(s32[64]{0:T(128)S(1)} %dynamic_slice.12.group_ref, f32[64]{0:T(128)S(1)} %dynamic-slice_bitcast_fusion.1.gain_ref, f32[4,2,1536,128]{3,2,1,0:T(8,128)} %get-tuple-element.8.raw_ref, f32[4,128,128]{2,1,0:T(8,128)S(1)} %get-tuple-element.9.v_ref, f32[12,96,256]{2,1,0:T(8,128)} %slice.20.tmpl_ref, ...), custom_call_target="tpu_custom_call" | custom-call | tf_op jit(solution)/shard_map/filter/pallas_call | solution.py:497
  253.8 0.0 copy-start
  253.8 2.8 %copy-done = f32[2,6144,128]{2,1,0:T(8,128)S(1)} copy-done((f32[2,6144,128]{2,1,0:T(8,128)S(1)}, f32[2,6144,128]{2,1,0:T(8,128)}, u32[]{:S(2)}) %copy-start) | copy-done | bytes 6291480
  256.6 2.6 unpack.1
  259.2 0.0 copy-start.2
  259.2 2.6 copy-done.2
  261.8 6.5 %copy.34 = f32[256,6000]{0,1:T(8,128)} copy(f32[256,6000]{1,0:T(8,128)} %copy-done.2) | data formatting | bytes 12288000
  268.4 0.2 copy.33
  268.6 1.0 reshape.38
  269.5 0.6 copy.41
  (7 shorter events, 0.2 us)
Async XLA Ops:
  2.7 2.1 copy-start.14
  4.8 1.6 copy-start.13
  4.8 1.8 copy-start.12
  14.3 2.7 %copy-start.3 = (f32[256,6000]{1,0:T(8,128)S(1)}, f32[256,6000]{1,0:T(8,128)}, u32[]{:S(2)}) copy-start(f32[256,6000]{1,0:T(8,128)} %copy.28.x_ref) | copy-start | bytes 18432004
  17.1 6.0 %copy-start.4 = (bf16[12,128,256]{2,1,0:T(8,128)(2,1)S(1)}, bf16[12,128,256]{2,1,0:T(8,128)(2,1)}, u32[]{:S(2)}) copy-start(bf16[12,128,256]{2,1,0:T(8,128)(2,1)} %constant.36.clone.e_ref) | copy-start | bytes 2359300
  17.1 6.0 %copy-start.10 = (s32[256]{0:T(256)S(1)}, s32[256]{0:T(256)}, u32[]{:S(2)}) copy-start(s32[256]{0:T(256)} %param.15) | copy-start | bytes 3076
  17.1 6.0 %copy-start.11 = (f32[256]{0:T(256)S(1)}, f32[256]{0:T(256)}, u32[]{:S(2)}) copy-start(f32[256]{0:T(256)} %param.17) | copy-start | bytes 3076
  20.4 2.6 copy-start.1
  172.8 1.6 copy-start.5
  172.8 2.0 copy-start.6
  172.8 1.9 copy-start.7
  172.8 1.9 copy-start.8
  172.9 1.9 copy-start.9
  253.8 2.8 %copy-start = (f32[2,6144,128]{2,1,0:T(8,128)S(1)}, f32[2,6144,128]{2,1,0:T(8,128)}, u32[]{:S(2)}) copy-start(f32[2,6144,128]{2,1,0:T(8,128)} %filter.1.y_ref) | copy-start | bytes 18874372
  259.2 2.6 copy-start.2

commit v3 on v2

--- a/solution.py
+++ b/solution.py
@@ -15,6 +15,7 @@
 GP = 16
 HALVES = QP // 128
 BAND = 32
+PIECES = 8
 CHUNK = 8
 MESH = pl.DeviceIdType.MESH
 F32 = jnp.float32
@@ -81,20 +82,29 @@
     pl.semaphore_wait(barrier, nd + nt - 2)
 
     waits = []
+    piece = share // PIECES
+
+    def send_piece(j):
+        for off in range(1, nt):
+            peer = tm_peer(off)
+            copy = pltpu.make_async_remote_copy(
+                src_ref=x_hbm.at[:, pl.ds(peer * share + j * piece, piece)],
+                dst_ref=raw_ref.at[tm, :, pl.ds(j * piece, piece)],
+                send_sem=raw_s.at[j, off], recv_sem=raw_r.at[j, off],
+                device_id=(det, peer), device_id_type=MESH)
+            copy.start()
+            waits.append(copy)
+
     for off in range(1, nt):
         peer = tm_peer(off)
-        copy = pltpu.make_async_remote_copy(
-            src_ref=x_hbm.at[:, pl.ds(peer * share, share)], dst_ref=raw_ref.at[tm],
-            send_sem=raw_s.at[off], recv_sem=raw_r.at[off],
-            device_id=(det, peer), device_id_type=MESH)
-        copy.start()
-        waits.append(copy)
         copy = pltpu.make_async_remote_copy(
             src_ref=vrc_ref.at[pl.ds(peer * vshare, vshare)], dst_ref=vraw_ref.at[tm],
             send_sem=val_s.at[off], recv_sem=val_r.at[off],
             device_id=(det, peer), device_id_type=MESH)
         copy.start()
         waits.append(copy)
+    for j in range(PIECES - 2 * ITERS):
+        send_piece(j)
     own_raw = pltpu.make_async_copy(x_hbm.at[:, pl.ds(tm * share, share)], raw_ref.at[tm], loc_sem.at[1])
     own_raw.start()
     own_val = pltpu.make_async_copy(vrc_ref.at[pl.ds(tm * vshare, vshare)], vraw_ref.at[tm], loc_sem.at[2])
@@ -157,6 +167,7 @@
                 device_id=(peer, tm), device_id_type=MESH)
             copy.start()
             copies.append(copy)
+        send_piece(PIECES - 2 * ITERS + 2 * it)
         weigh(det)
         for copy in copies:
             copy.wait_recv()
@@ -187,6 +198,7 @@
                 device_id=(det_peer(off), tm), device_id_type=MESH)
             copy.start()
             gather.append(copy)
+        send_piece(PIECES - 2 * ITERS + 2 * it + 1)
         for off in range(1, nd):
             source = lax.rem(det + nd - off, nd)
             pltpu.make_async_remote_copy(
@@ -465,7 +477,7 @@
             pltpu.VMEM((ITERS, nd, cycles, GP, 128), F32),
             pltpu.VMEM((ITERS, padded, GP, QP), F32),
             pltpu.VMEM((ITERS, nt, 8, rows), F32),
-            dma((4,)), dma((nt,)), dma((nt,)), dma((nt,)), dma((nt,)),
+            dma((4,)), dma((PIECES, nt)), dma((PIECES, nt)), dma((nt,)), dma((nt,)),
             dma((ITERS, nd)), dma((ITERS, nd)), dma((ITERS, nd)), dma((ITERS, nd)),
             dma((ITERS, nd)), dma((ITERS, nd)), dma((ITERS, nt)), dma((ITERS, nt)),
             dma((nt,)), dma((nt,)),

time: 271 us -> 237 us (0.87)
  Pallas kernels: 234 us -> 200 us
    pallas_call x1, Pallas kernels: 149 us -> 115 us  [local(): pl.pallas_call(functools.partial(fit_kernel, nd, nt, slabs, own, cyc, row...]
where the time goes in v3:
time: 237 us
  Pallas kernels  200 us (84%)
  local copies, waits for them, and re-layouts  32.1 us (14%)
  matrix products  2.45 us (1%)
    pallas_call x1, Pallas kernels, local(): pl.pallas_call(functools.partial(fit_kernel, nd, nt, slabs, own, cyc, row...  115 us
    pallas_call x1, Pallas kernels, local(): pl.pallas_call(functools.partial(filter_kernel, nt, slabs, cyc, count, ha...  79 us
    unnamed x34, local copies, waits for them, and re-layouts  25.7 us

profile of v3, /device:TPU:13, one launch (start us, length us, event | category | flops | bytes accessed | tf_op | source)
XLA Modules:
  0.0 236.7 jit_solution(17306265273710485923)
XLA Ops:
  0.6 0.8 dynamic_slice.12.group_ref
  1.4 0.8 convert_element_type.12
  2.2 0.1 copy.29
  2.4 0.2 copy.39
  2.6 0.1 pad.8.clone
  2.7 0.0 copy-start.14
  2.7 2.1 reshape.36
  4.8 0.0 copy-done.14
  4.8 0.0 copy-start.13
  4.8 0.0 copy-start.12
  4.9 1.5 convolution_bitcast_fusion
  6.4 0.0 copy-done.13
  6.4 0.2 fusion.2
  6.7 0.0 copy-done.12
  6.7 0.7 fusion
  7.5 0.1 maximum_add_fusion.w_ref
  7.6 6.7 %copy.28.x_ref = f32[256,6000]{1,0:T(8,128)} copy(f32[256,6000]{0,1:T(8,128)} %param.14) | data formatting | bytes 12288000 | tf_op args[0]
  14.3 0.0 copy-start.3
  14.3 2.7 %copy-done.3 = f32[256,6000]{1,0:T(8,128)S(1)} copy-done((f32[256,6000]{1,0:T(8,128)S(1)}, f32[256,6000]{1,0:T(8,128)}, u32[]{:S(2)}) %copy-start.3) | copy-done | bytes 6144024
  17.1 0.0 copy-start.4
  17.1 0.0 copy-start.10
  17.1 0.0 copy-start.11
  17.1 3.3 %pack.1.x_hbm = f32[2,6144,128]{2,1,0:T(8,128)S(1)} custom-call(f32[256,6000]{1,0:T(8,128)S(1)} %copy-done.3), custom_call_target="tpu_custom_call" | custom-call | tf_op jit(solution)/shard_map/pack/pallas_call | solution.py:443
  20.4 0.0 copy-start.1
  20.4 2.6 %copy-done.1 = f32[2,6144,128]{2,1,0:T(8,128)} copy-done((f32[2,6144,128]{2,1,0:T(8,128)}, f32[2,6144,128]{2,1,0:T(8,128)S(1)}, u32[]{:S(2)}) %copy-start.1) | copy-done | bytes 6291480
  23.1 0.0 copy-done.4
  23.1 0.0 copy-done.10
  23.1 0.0 copy-done.11
  23.1 115.3 %fit.1 = (f32[4,2,1536,128]{3,2,1,0:T(8,128)}, f32[4,128,128]{2,1,0:T(8,128)S(1)}, f32[4,24,16,256]{3,2,1,0:T(8,128)S(1)}, f32[1,256]{1,0:T(1,128)S(1)}) custom-call(f32[2,6144,128]{2,1,0:T(8,128)} %copy-done.1, bf16[2,256,128]{2,1,0:T(8,128)(2,1)S(1)} %convert_bitcast_fusion.v_ref, f32[512,128]{1,0:T(8,128)S(1)} %bitcast.28, s32[1,256]{1,0:T(1,128)S(1)} %bitcast.29, ...), custom_call_target="tpu_custom_call" | custom-call | tf_op jit(solution)/shard_map/fit/pallas_call | solution.py:460
  138.4 0.1 dynamic-slice_bitcast_fusion.1.gain_ref
  138.5 0.9 copy.31
  139.4 0.0 copy-start.5
  139.4 0.0 copy-start.6
  139.5 0.0 copy-start.7
  139.5 0.0 copy-start.8
  139.5 0.0 copy-start.9
  139.5 1.1 slice.20.tmpl_ref
  140.6 0.5 copy-done.5
  141.1 0.3 copy-done.6
  141.4 0.0 copy-done.7
  141.4 0.0 copy-done.8
  141.4 0.0 copy-done.9
  141.4 79.0 %filter.1.y_ref = f32[2,6144,128]{2,1,0:T(8,128)} custom-call(s32[64]{0:T(128)S(1)} %dynamic_slice.12.group_ref, f32[64]{0:T(128)S(1)} %dynamic-slice_bitcast_fusion.1.gain_ref, f32[4,2,1536,128]{3,2,1,0:T(8,128)} %get-tuple-element.8.raw_ref, f32[4,128,128]{2,1,0:T(8,128)S(1)} %get-tuple-element.9.v_ref, f32[12,96,256]{2,1,0:T(8,128)} %slice.20.tmpl_ref, ...), custom_call_target="tpu_custom_call" | custom-call | tf_op jit(solution)/shard_map/filter/pallas_call | solution.py:509
  220.4 0.0 copy-start
  220.4 2.8 %copy-done = f32[2,6144,128]{2,1,0:T(8,128)S(1)} copy-done((f32[2,6144,128]{2,1,0:T(8,128)S(1)}, f32[2,6144,128]{2,1,0:T(8,128)}, u32[]{:S(2)}) %copy-start) | copy-done | bytes 6291480
  223.2 2.6 %unpack.1 = f32[256,6000]{1,0:T(8,128)S(1)} custom-call(f32[2,6144,128]{2,1,0:T(8,128)S(1)} %copy-done), custom_call_target="tpu_custom_call" | custom-call | tf_op jit(solution)/shard_map/unpack/pallas_call | solution.py:526
  225.8 0.0 copy-start.2
  225.8 2.6 %copy-done.2 = f32[256,6000]{1,0:T(8,128)} copy-done((f32[256,6000]{1,0:T(8,128)}, f32[256,6000]{1,0:T(8,128)S(1)}, u32[]{:S(2)}) %copy-start.2) | copy-done | bytes 6144024
  228.4 6.5 %copy.34 = f32[256,6000]{0,1:T(8,128)} copy(f32[256,6000]{1,0:T(8,128)} %copy-done.2) | data formatting | bytes 12288000
  235.0 0.2 copy.33
  235.2 1.0 reshape.38
  236.1 0.6 copy.41
  (7 shorter events, 0.2 us)
Async XLA Ops:
  2.7 2.1 copy-start.14
  4.8 1.6 copy-start.13
  4.8 1.8 copy-start.12
  14.3 2.7 %copy-start.3 = (f32[256,6000]{1,0:T(8,128)S(1)}, f32[256,6000]{1,0:T(8,128)}, u32[]{:S(2)}) copy-start(f32[256,6000]{1,0:T(8,128)} %copy.28.x_ref) | copy-start | bytes 18432004
  17.1 6.0 %copy-start.4 = (bf16[12,128,256]{2,1,0:T(8,128)(2,1)S(1)}, bf16[12,128,256]{2,1,0:T(8,128)(2,1)}, u32[]{:S(2)}) copy-start(bf16[12,128,256]{2,1,0:T(8,128)(2,1)} %constant.36.clone.e_ref) | copy-start | bytes 2359300
  17.1 6.0 %copy-start.10 = (s32[256]{0:T(256)S(1)}, s32[256]{0:T(256)}, u32[]{:S(2)}) copy-start(s32[256]{0:T(256)} %param.15) | copy-start | bytes 3076
  17.1 6.0 %copy-start.11 = (f32[256]{0:T(256)S(1)}, f32[256]{0:T(256)}, u32[]{:S(2)}) copy-start(f32[256]{0:T(256)} %param.17) | copy-start | bytes 3076
  20.4 2.6 %copy-start.1 = (f32[2,6144,128]{2,1,0:T(8,128)}, f32[2,6144,128]{2,1,0:T(8,128)S(1)}, u32[]{:S(2)}) copy-start(f32[2,6144,128]{2,1,0:T(8,128)S(1)} %pack.1.x_hbm) | copy-start | bytes 18874372
  139.4 1.6 copy-start.5
  139.4 2.0 copy-start.6
  139.5 1.9 copy-start.7
  139.5 1.9 copy-start.8
  139.5 1.9 copy-start.9
  220.4 2.8 %copy-start = (f32[2,6144,128]{2,1,0:T(8,128)S(1)}, f32[2,6144,128]{2,1,0:T(8,128)}, u32[]{:S(2)}) copy-start(f32[2,6144,128]{2,1,0:T(8,128)} %filter.1.y_ref) | copy-start | bytes 18874372
  225.8 2.6 %copy-start.2 = (f32[256,6000]{1,0:T(8,128)}, f32[256,6000]{1,0:T(8,128)S(1)}, u32[]{:S(2)}) copy-start(f32[256,6000]{1,0:T(8,128)S(1)} %unpack.1) | copy-start | bytes 18432004

commit v4 on v3

--- a/solution.py
+++ b/solution.py
@@ -14,7 +14,7 @@
 QP = 256
 GP = 16
 HALVES = QP // 128
-BAND = 32
+BAND = 128
 PIECES = 8
 CHUNK = 8
 MESH = pl.DeviceIdType.MESH
@@ -43,16 +43,15 @@
 
 def pack_kernel(slabs, x_ref, out_ref):
     for p in range(slabs):
-        wide = x_ref[:, Q * p:Q * (p + 1)]
-        wide = jnp.concatenate([wide, jnp.zeros((BAND, QP - Q), F32)], axis=1)
+        tall = jnp.concatenate([x_ref[Q * p:Q * (p + 1), :], jnp.zeros((QP - Q, BAND), F32)], axis=0)
         for h in range(HALVES):
-            out_ref[h, pl.ds(p, BAND, stride=slabs), :] = wide[:, 128 * h:128 * (h + 1)]
+            out_ref[h, pl.ds(p, BAND, stride=slabs), :] = tall[128 * h:128 * (h + 1)].T
 
 
 def unpack_kernel(slabs, y_ref, out_ref):
     for p in range(slabs):
-        wide = jnp.concatenate([y_ref[h, pl.ds(p, BAND, stride=slabs), :] for h in range(HALVES)], axis=1)
-        out_ref[:, Q * p:Q * (p + 1)] = wide[:, :Q]
+        tall = jnp.concatenate([y_ref[h, pl.ds(p, BAND, stride=slabs), :].T for h in range(HALVES)], axis=0)
+        out_ref[Q * p:Q * (p + 1), :] = tall[:Q]
 
 
 def fit_kernel(nd, nt, slabs, own, cyc, rows,
@@ -444,11 +443,11 @@
         functools.partial(pack_kernel, slabs),
         out_shape=jax.ShapeDtypeStruct((HALVES, rows * slabs, 128), F32),
         grid=(rows // BAND,),
-        in_specs=[pl.BlockSpec((BAND, samp), lambda i: (i, 0))],
+        in_specs=[pl.BlockSpec((samp, BAND), lambda i: (0, i))],
         out_specs=pl.BlockSpec((HALVES, BAND * slabs, 128), lambda i: (0, i, 0)),
         compiler_params=pltpu.CompilerParams(vmem_limit_bytes=32 * 2**20),
         name="pack",
-    )(timestreams)
+    )(timestreams.T)
     vrc = jnp.pad(valid_blocks.astype(F32).reshape(rows, cycles, per), ((0, 0), (0, 0), (0, 128 - per)))
     v = jnp.transpose(vrc, (1, 0, 2)).astype(BF16)
     vrc = vrc.reshape(rows * cycles, 128)
@@ -525,13 +524,13 @@
       jnp.asarray(f1), jnp.asarray(tw), jnp.asarray(m2), jnp.asarray(m3), jnp.asarray(f4))
     filtered = pl.pallas_call(
         functools.partial(unpack_kernel, slabs),
-        out_shape=jax.ShapeDtypeStruct((rows, samp), F32),
+        out_shape=jax.ShapeDtypeStruct((samp, rows), F32),
         grid=(rows // BAND,),
         in_specs=[pl.BlockSpec((HALVES, BAND * slabs, 128), lambda i: (0, i, 0))],
-        out_specs=pl.BlockSpec((BAND, samp), lambda i: (i, 0)),
+        out_specs=pl.BlockSpec((samp, BAND), lambda i: (0, i)),
         compiler_params=pltpu.CompilerParams(vmem_limit_bytes=32 * 2**20),
         name="unpack",
-    )(out)
+    )(out).T
     return (filtered, gains, template)
 
 

time: 237 us -> 222 us (0.937)
  local copies, waits for them, and re-layouts: 32.1 us -> 14.8 us
    unnamed x34 -> x32, local copies, waits for them, and re-layouts: 25.7 us -> 7.07 us
where the time goes in v4:
time: 222 us
  Pallas kernels  201 us (91%)
  local copies, waits for them, and re-layouts  14.8 us (7%)
  matrix products  4.01 us (2%)
    pallas_call x1, Pallas kernels, local(): pl.pallas_call(functools.partial(fit_kernel, nd, nt, slabs, own, cyc, row...  115 us
    pallas_call x1, Pallas kernels, local(): pl.pallas_call(functools.partial(filter_kernel, nt, slabs, cyc, count, ha...  79 us
    unnamed x32, local copies, waits for them, and re-layouts  7.07 us

profile of v4, /device:TPU:13, one launch (start us, length us, event | category | flops | bytes accessed | tf_op | source)
XLA Modules:
  0.0 222.1 jit_solution(3791576046786741372)
XLA Ops:
  0.6 0.8 dynamic_slice.12.group_ref
  1.4 0.8 convert_element_type.12
  2.2 0.1 copy.24
  2.4 0.2 copy.33
  2.6 0.1 pad.8.clone
  2.7 0.0 copy-start.12
  2.7 0.0 copy-start.11
  2.7 0.0 copy-start.10
  2.8 0.0 slice-start
  2.8 3.4 %reshape.36 = f32[12,250,96]{2,1,0:T(8,128)} reshape(f32[12,24000]{1,0:T(8,128)} %param.18) | data formatting | bytes 2304000 | tf_op jit(solution)/shard_map/reshape | solution.py:498
  6.1 0.0 copy-done.12
  6.1 0.0 slice-start.1
  6.1 3.1 %convolution_bitcast_fusion = f32[12,112,250]{2,1,0:T(8,128)S(1)} fusion(f32[96,112,1]{1,0,2:T(8,128)S(1)} %copy-done.12, f32[12,250,96]{2,1,0:T(8,128)} %reshape.36), kind=kOutput, calls=%fused_computation | convolution fusion | flops 387072000 | bytes 2539008 | tf_op jit(solution)/shard_map/gjp,pk->gkj/dot_general | solution.py:498
  9.3 0.0 copy-done.11
  9.3 0.2 fusion.2
  9.5 0.0 copy-done.10
  9.5 0.7 fusion
  10.3 0.1 maximum_add_fusion.w_ref
  10.4 0.0 slice-done
  10.4 0.0 slice-done.1
  10.4 0.0 copy-start.2
  10.5 0.0 copy-start.8
  10.5 0.0 copy-start.9
  10.5 3.1 %pack.1.x_hbm = f32[2,6144,128]{2,1,0:T(8,128)S(1)} custom-call(f32[6000,256]{1,0:T(8,128)S(1)} %bitcast.32), custom_call_target="tpu_custom_call" | custom-call | tf_op jit(solution)/shard_map/pack/pallas_call | solution.py:442
  13.6 0.0 copy-start.1
  13.6 2.6 %copy-done.1 = f32[2,6144,128]{2,1,0:T(8,128)} copy-done((f32[2,6144,128]{2,1,0:T(8,128)}, f32[2,6144,128]{2,1,0:T(8,128)S(1)}, u32[]{:S(2)}) %copy-start.1) | copy-done | bytes 6291480
  16.3 0.0 copy-done.2
  16.3 0.0 copy-done.8
  16.3 0.0 copy-done.9
  16.3 115.3 %fit.1 = (f32[4,2,1536,128]{3,2,1,0:T(8,128)}, f32[4,128,128]{2,1,0:T(8,128)S(1)}, f32[4,24,16,256]{3,2,1,0:T(8,128)S(1)}, f32[1,256]{1,0:T(1,128)S(1)}) custom-call(f32[2,6144,128]{2,1,0:T(8,128)} %copy-done.1, bf16[2,256,128]{2,1,0:T(8,128)(2,1)S(1)} %convert_bitcast_fusion.v_ref, f32[512,128]{1,0:T(8,128)S(1)} %bitcast.33, s32[1,256]{1,0:T(1,128)S(1)} %bitcast.34, ...), custom_call_target="tpu_custom_call" | custom-call | tf_op jit(solution)/shard_map/fit/pallas_call | solution.py:459
  131.6 0.1 dynamic-slice_bitcast_fusion.1.gain_ref
  131.7 0.9 copy.26
  132.6 0.0 copy-start.3
  132.6 0.0 copy-start.4
  132.7 0.0 copy-start.5
  132.7 0.0 copy-start.6
  132.7 0.0 copy-start.7
  132.7 1.1 slice.20.tmpl_ref
  133.8 0.5 copy-done.3
  134.3 0.3 copy-done.4
  134.6 0.0 copy-done.5
  134.6 0.0 copy-done.6
  134.6 0.0 copy-done.7
  134.6 79.0 %filter.1.y_ref = f32[2,6144,128]{2,1,0:T(8,128)} custom-call(s32[64]{0:T(128)S(1)} %dynamic_slice.12.group_ref, f32[64]{0:T(128)S(1)} %dynamic-slice_bitcast_fusion.1.gain_ref, f32[4,2,1536,128]{3,2,1,0:T(8,128)} %get-tuple-element.8.raw_ref, f32[4,128,128]{2,1,0:T(8,128)S(1)} %get-tuple-element.9.v_ref, f32[12,96,256]{2,1,0:T(8,128)} %slice.20.tmpl_ref, ...), custom_call_target="tpu_custom_call" | custom-call | tf_op jit(solution)/shard_map/filter/pallas_call | solution.py:508
  213.6 0.0 copy-start
  213.6 2.8 %copy-done = f32[2,6144,128]{2,1,0:T(8,128)S(1)} copy-done((f32[2,6144,128]{2,1,0:T(8,128)S(1)}, f32[2,6144,128]{2,1,0:T(8,128)}, u32[]{:S(2)}) %copy-start) | copy-done | bytes 6291480
  216.4 4.0 %unpack.1 = f32[6000,256]{1,0:T(8,128)} custom-call(f32[2,6144,128]{2,1,0:T(8,128)S(1)} %copy-done), custom_call_target="tpu_custom_call" | custom-call | tf_op jit(solution)/shard_map/unpack/pallas_call | solution.py:525
  220.4 0.2 copy.28
  220.6 1.0 reshape.38
  221.5 0.6 copy.35
  (8 shorter events, 0.2 us)
Async XLA Ops:
  2.7 3.4 %copy-start.12 = (f32[96,112,1]{1,0,2:T(8,128)S(1)}, f32[96,112,1]{1,0,2:T(8,128)}, u32[]{:S(2)}) copy-start(f32[96,112,1]{1,0,2:T(8,128)} %constant.50) | copy-start | bytes 129028
  2.7 6.5 %copy-start.11 = (f32[250,256]{1,0:T(8,128)S(1)}, f32[250,256]{1,0:T(8,128)}, u32[]{:S(2)}) copy-start(f32[250,256]{1,0:T(8,128)} %constant.38.clone) | copy-start | bytes 768004
  2.7 6.8 %copy-start.10 = (f32[250,256,1]{1,0,2:T(8,128)S(1)}, f32[250,256,1]{1,0,2:T(8,128)}, u32[]{:S(2)}) copy-start(f32[250,256,1]{1,0,2:T(8,128)} %constant.51) | copy-start | bytes 768004
  2.8 7.7 %slice-start = ((s8[6144000]{0:T(1024)(128)(4,1)}), s8[1949696]{0:T(1024)(128)(4,1)S(1)}, s32[]{:S(2)}) async-start(s8[6144000]{0:T(1024)(128)(4,1)} %bitcast.30), calls=%async_computation | async-start | bytes 3899392
  6.1 4.3 %slice-start.1 = ((s8[6144000]{0:T(1024)(128)(4,1)}), s8[4194304]{0:T(1024)(128)(4,1)S(1)}, s32[]{:S(2)}) async-start(s8[6144000]{0:T(1024)(128)(4,1)} %bitcast.30), calls=%async_computation.1 | async-start | bytes 8388608
  10.4 5.8 %copy-start.2 = (bf16[12,128,256]{2,1,0:T(8,128)(2,1)S(1)}, bf16[12,128,256]{2,1,0:T(8,128)(2,1)}, u32[]{:S(2)}) copy-start(bf16[12,128,256]{2,1,0:T(8,128)(2,1)} %constant.36.clone.e_ref) | copy-start | bytes 2359300
  10.5 5.8 %copy-start.8 = (s32[256]{0:T(256)S(1)}, s32[256]{0:T(256)}, u32[]{:S(2)}) copy-start(s32[256]{0:T(256)} %param.15) | copy-start | bytes 3076
  10.5 5.8 %copy-start.9 = (f32[256]{0:T(256)S(1)}, f32[256]{0:T(256)}, u32[]{:S(2)}) copy-start(f32[256]{0:T(256)} %param.17) | copy-start | bytes 3076
  13.6 2.6 %copy-start.1 = (f32[2,6144,128]{2,1,0:T(8,128)}, f32[2,6144,128]{2,1,0:T(8,128)S(1)}, u32[]{:S(2)}) copy-start(f32[2,6144,128]{2,1,0:T(8,128)S(1)} %pack.1.x_hbm) | copy-start | bytes 18874372
  132.6 1.6 copy-start.3
  132.6 2.0 copy-start.4
  132.7 1.9 copy-start.5
  132.7 1.9 copy-start.6
  132.7 1.9 copy-start.7
  213.6 2.8 %copy-start = (f32[2,6144,128]{2,1,0:T(8,128)S(1)}, f32[2,6144,128]{2,1,0:T(8,128)}, u32[]{:S(2)}) copy-start(f32[2,6144,128]{2,1,0:T(8,128)} %filter.1.y_ref) | copy-start | bytes 18874372
